TPU v7x, 512 devices: a whole 4x8x8 slice. The times are simulated.
512 devices in a mesh: blk: 128 (over z, y, core), ga: 4 (over x).
Axes of the slice: x: 4, y: 8, z: 8, core: 2. Of those that a mesh axis runs over, the one named last changes fastest.
Arguments:
- thermal_deviation: bfloat16 [32768, 128], P('blk', 'ga'), may hold values from -4 to 4
- moisture_mass: bfloat16 [32768, 128], P('blk', 'ga'), may hold values from 0.19921875 to 2
- condensate_optic: bfloat16 [32768, 128], P('blk', 'ga'), may hold values from 0.0099487305 to 1
- sun_height_factor: float32 [32768], P('blk'), may hold values from -1 to 1
- group_assignment: int32 [32768], P('blk'), may hold values from 0 to 127, as said below
- opacity_factor: float32 [256], P('ga'), may hold values from 0.001 to 0.03
- thermal_power: float32 [256], P('ga'), may hold values from -2 to 2
- sunlight_weights: float32 [256], P('ga'), may hold values from 0.2 to 2
- thermal_weights: float32 [256], P('ga'), may hold values from 0.05 to 0.5
Outputs:
- heating: float32 [32768, 128], P('blk', 'ga')
- surface: float32 [32768], P(('blk', 'ga'))
Inputs may be any that keep to these rules, and one draw needn't show every extreme that they name: `group_assignment`: each dynamics block of 256 columns names every group exactly 2 times.
All inputs are finite; a program needn't handle non-finite values.
Results may differ from a plain program's by a relative error of at most 0.0013.
Values may be sent and summed in bfloat16 or wider, within the bound.
A program may use at most 64 MiB of HBM per device.

v0:
```python
import jax
import jax.numpy as jnp
from jax import lax
from jax.sharding import PartitionSpec as P


def optical_depths(
    t, w, c, solar_elevation_factor, coefficient_entry, planck_entry, sunlight_entry, physics_entry
):
    tau = coefficient_entry[:, None, None] * (
        w[None] * jnp.exp(planck_entry[:, None, None] * t[None]) + c[None]
    )
    depth = 1.66 * jnp.cumsum(tau, axis=2)
    trans = jnp.exp(-depth)
    ones_col = jnp.ones(trans.shape[:2] + (1,), jnp.float32)
    above = jnp.concatenate([ones_col, trans[:, :, :-1]], axis=2)
    solar_part = (
        sunlight_entry[:, None, None] * solar_elevation_factor[None, :, None] * (above - trans)
    )
    emitted = physics_entry[:, None, None] * (1.0 + 0.2 * t[None]) * (1.0 - jnp.exp(-1.66 * tau))
    warming_rate = 0.0625 * jnp.sum(solar_part - emitted, axis=0)
    ground_flux = jnp.sum(
        sunlight_entry[:, None] * solar_elevation_factor[None, :] * trans[:, :, -1], axis=0
    )
    return (warming_rate, ground_flux)


def compute_radiation(
    thermal_column,
    absorbing_mass,
    overcast_share,
    solar_elevation_factor,
    opacity_factor,
    thermal_power,
    sunlight_weights,
    thermal_weights,
):
    vertical_stacks, layer_number = thermal_column.shape
    group_sequence = opacity_factor.shape[0] // 8

    def step(carry, radiative_settings):
        coefficient_entry, planck_entry, sunlight_entry, physics_entry = radiative_settings
        warming_rate, ground_flux = optical_depths(
            thermal_column,
            absorbing_mass,
            overcast_share,
            solar_elevation_factor,
            coefficient_entry,
            planck_entry,
            sunlight_entry,
            physics_entry,
        )
        return ((carry[0] + warming_rate, carry[1] + ground_flux), None)

    start = (
        jnp.zeros((vertical_stacks, layer_number), jnp.float32),
        jnp.zeros((vertical_stacks,), jnp.float32),
    )
    radiative_settings = (
        opacity_factor.reshape(group_sequence, 8),
        thermal_power.reshape(group_sequence, 8),
        sunlight_weights.reshape(group_sequence, 8),
        thermal_weights.reshape(group_sequence, 8),
    )
    (heat_part, surf_part), unused = lax.scan(step, start, radiative_settings)
    return (heat_part, surf_part)


def shards(
    thermal_deviation,
    moisture_mass,
    condensate_optic,
    sun_height_factor,
    group_assignment,
    opacity_factor,
    thermal_power,
    sunlight_weights,
    thermal_weights,
):
    nblock = lax.axis_size("blk")
    nshare = lax.axis_size("ga")
    vertical_stacks = group_assignment.shape[0]
    per = vertical_stacks // nblock
    quarter = thermal_deviation.shape[1]
    order = jnp.argsort(group_assignment, stable=True)
    inverse = jnp.argsort(order)
    state = jnp.stack([thermal_deviation[order], moisture_mass[order]])
    moved = lax.all_to_all(
        state.reshape(2, nblock, per, quarter), "blk", split_axis=1, concat_axis=1, tiled=True
    )
    moved = moved.reshape(2, vertical_stacks, quarter)
    whole, condensate_field = (
        lax.all_gather(moved, "ga", axis=2, tiled=True),
        lax.all_gather(condensate_optic, "ga", axis=1, tiled=True),
    )
    solar_elevation_factor = jnp.maximum(sun_height_factor, 0.0)
    heat_part, surf_part = compute_radiation(
        whole[0].astype(jnp.float32),
        whole[1].astype(jnp.float32),
        condensate_field.astype(jnp.float32),
        solar_elevation_factor,
        opacity_factor,
        thermal_power,
        sunlight_weights,
        thermal_weights,
    )
    heat_all, surf_all = lax.psum((heat_part, surf_part), "ga")
    index = lax.axis_index("ga")
    heat_mine = lax.dynamic_slice_in_dim(heat_all, index * quarter, quarter, 1)
    surface = lax.dynamic_slice_in_dim(
        surf_all, index * (vertical_stacks // nshare), vertical_stacks // nshare, 0
    )
    back = lax.all_to_all(
        heat_mine.reshape(nblock, per, quarter), "blk", split_axis=0, concat_axis=0, tiled=True
    )
    heating = back.reshape(vertical_stacks, quarter)[inverse]
    return (heating, surface)


def solution(mesh):
    in_specs = (
        P("blk", "ga"),
        P("blk", "ga"),
        P("blk", "ga"),
        P("blk"),
        P("blk"),
        P("ga"),
        P("ga"),
        P("ga"),
        P("ga"),
    )
    out_specs = (P("blk", "ga"), P(("blk", "ga")))
    return jax.shard_map(shards, mesh=mesh, in_specs=in_specs, out_specs=out_specs, check_vma=False)
```

profile of v0, /device:TPU:1, one launch (start us, length us, event | category | flops | bytes accessed | tf_op | source)
XLA Modules:
  0.0 166.4 jit_solution(14499094843094120690)
XLA Ops:
  7.2 0.7 copy-done.3
  7.8 3.2 %sort.34 = (s32[256]{0:T(256)}, s32[256]{0:T(256)S(1)}) sort(s32[256]{0:T(256)S(1)} %copy-done.3, s32[256]{0:T(256)S(1)} %iota.8), dimensions={0}, to_apply=%region_0.0 | sort | flops 2048 | bytes 4096 | tf_op jit(solution)/shard_map/jit(argsort)/sort | solution.py:85
  11.0 0.8 copy.37
  12.0 0.9 gather_fusion
  12.9 0.9 gather_fusion.1
  13.7 0.9 pad_maximum_fusion
  14.6 18.6 %all-to-all-start = ((bf16[2,128,2,32]{3,2,0,1:T(2,128)(2,1)}), bf16[2,128,2,32]{3,2,0,1:T(2,128)(2,1)S(1)}, u32[]{:S(2)}, u32[]{:S(2)}) async-start(bf16[2,128,2,32]{3,2,0,1:T(2,128)(2,1)} %pad_maximum_fusion), calls=%async_computation | async-start | bytes 262144 | tf_op jit(solution)/shard_map/all_to_all | solution.py:88
  33.2 10.2 %all_gather.7 = bf16[256,128]{0,1:T(8,128)(2,1)S(1)} all-gather(bf16[256,32]{0,1:T(8,128)(2,1)S(1)} %copy-done.2), channel_id=1, replica_groups=mesh['blk'=128,'ga'=4] {'ga'}, dimensions={1}, use_global_device_ids=true | all-gather | bytes 81920 | tf_op jit(solution)/shard_map/all_gather | solution.py:94
  43.5 0.6 copy-done.5
  44.2 0.6 copy-done.6
  44.8 0.6 copy-done.7
  46.2 3.2 %sort.35 = (s32[256]{0:T(256)}, s32[256]{0:T(256)S(1)}) sort(s32[256]{0:T(256)S(1)} %get-tuple-element.62, s32[256]{0:T(256)S(1)} %iota.9), dimensions={0}, to_apply=%region_7.8 | sort | flops 2048 | bytes 4096 | tf_op jit(solution)/shard_map/jit(argsort)/sort | solution.py:86
  49.5 9.1 %all_gather.6 = bf16[2,256,128]{1,0,2:T(2,128)(2,1)S(1)} all-gather(bf16[2,256,32]{1,0,2:T(2,128)(2,1)S(1)} %copy.42), channel_id=1, replica_groups=mesh['blk'=128,'ga'=4] {'ga'}, dimensions={2}, use_global_device_ids=true | all-gather | bytes 163840 | tf_op jit(solution)/shard_map/all_gather | solution.py:93
  58.9 13.0 %while.13 = (s32[]{:T(128)}, f32[256,128]{0,1:T(8,128)S(1)}, f32[256]{0:T(256)S(1)}, f32[8,8]{1,0:T(8,128)S(1)}, f32[256]{0:T(256)S(1)}, /*index=5*/f32[8,8]{1,0...) while((s32[]{:T(128)}, f32[256,128]{0,1:T(8,128)S(1)}, ...), condition=%wide.region_5.6_spmd.clone, body=%wide.region_1.5_spmd.clone.sunk | while | flops 38148352 | bytes 6952528 | solution.py:65
  59.5 0.9 subtract_reduce_fusion.2
  61.1 0.9 subtract_reduce_fusion.2
  62.8 0.9 subtract_reduce_fusion.2
  64.4 0.9 subtract_reduce_fusion.2
  66.0 0.9 subtract_reduce_fusion.2
  67.6 0.9 subtract_reduce_fusion.2
  69.3 0.9 subtract_reduce_fusion.2
  70.9 0.9 subtract_reduce_fusion.2
  71.9 0.6 copy-done
  72.5 55.0 %all-reduce.3.cloned.1.call-done = f32[256,128]{0,1:T(8,128)} async-done(((f32[256,128]{0,1:T(8,128)}), f32[256,128]{0,1:T(8,128)}) %all-reduce.3.cloned.1.call-update) | async-done | bytes 131088 | tf_op jit(solution)/shard_map/psum | solution.py:107
  127.5 0.8 constant_dynamic-slice_fusion.4
  128.3 0.7 copy.43
  129.0 16.4 %all-to-all-start.1 = ((f32[128,2,32]{2,1,0:T(2,128)}), f32[128,2,32]{2,1,0:T(2,128)S(1)}, u32[]{:S(2)}, u32[]{:S(2)}) async-start(f32[128,2,32]{2,1,0:T(2,128)} %bitcast.5), calls=%async_computation.1 | async-start | bytes 262144 | tf_op jit(solution)/shard_map/all_to_all | solution.py:113
  145.4 7.9 %psum.15 = f32[256]{0:T(256)S(1)} all-reduce(f32[256]{0:T(256)S(1)} %get-tuple-element.65), channel_id=1, replica_groups=mesh['blk'=128,'ga'=4] {'ga'}, use_global_device_ids=true, to_apply=%region_8.9 | all-reduce | flops 256 | bytes 2048 | tf_op jit(solution)/shard_map/psum | solution.py:107
  153.3 0.6 dynamic_slice.20
  153.9 4.2 %all-to-all-done.1 = f32[128,2,32]{2,1,0:T(2,128)S(1)} async-done(((f32[128,2,32]{2,1,0:T(2,128)}), f32[128,2,32]{2,1,0:T(2,128)S(1)}, u32[]{:S(2)}, u32[]{:S(2)}) %all-to-all-start.1) | async-done | bytes 32800 | tf_op jit(solution)/shard_map/all_to_all | solution.py:113
  158.1 0.7 gather_fusion.2
  158.9 0.7 copy.44
  (99 shorter events, 6.8 us)
Async XLA Ops:
  7.2 0.7 copy-start.3
  11.0 0.9 copy-start.1
  14.6 18.6 %copy-start.4 = (f32[256]{0:T(256)S(1)}, f32[256]{0:T(256)}, u32[]{:S(2)}) copy-start(f32[256]{0:T(256)} %param.14) | copy-start | bytes 3076
  14.6 18.7 %copy-start.2 = (bf16[256,32]{0,1:T(8,128)(2,1)S(1)}, bf16[256,32]{0,1:T(8,128)(2,1)}, u32[]{:S(2)}) copy-start(bf16[256,32]{0,1:T(8,128)(2,1)} %param.13) | copy-start | bytes 49156
  14.6 34.8 %all-to-all-start = ((bf16[2,128,2,32]{3,2,0,1:T(2,128)(2,1)}), bf16[2,128,2,32]{3,2,0,1:T(2,128)(2,1)S(1)}, u32[]{:S(2)}, u32[]{:S(2)}) async-start(bf16[2,128,2,32]{3,2,0,1:T(2,128)(2,1)} %pad_maximum_fusion), calls=%async_computation | async-start | bytes 262144 | tf_op jit(solution)/shard_map/all_to_all | solution.py:88
  33.1 94.4 %all-reduce.3.cloned.1.call-start = ((), (), s32[]{:S(2)}) async-start(), calls=%async_computation.2 | async-start | bytes 262144 | tf_op jit(solution)/shard_map/psum | solution.py:107
  43.5 0.7 copy-start.5
  44.1 0.7 copy-start.6
  44.8 0.7 copy-start.7
  45.4 0.7 copy-start.8
  71.9 0.7 copy-start
  129.0 29.1 %all-to-all-start.1 = ((f32[128,2,32]{2,1,0:T(2,128)}), f32[128,2,32]{2,1,0:T(2,128)S(1)}, u32[]{:S(2)}, u32[]{:S(2)}) async-start(f32[128,2,32]{2,1,0:T(2,128)} %bitcast.5), calls=%async_computation.1 | async-start | bytes 262144 | tf_op jit(solution)/shard_map/all_to_all | solution.py:113
Sparse Core Ops, SparseCore 0:
  72.7 54.8 all-reduce.2
where the time goes:
time: 167 us; the launch traced here: 166 us
  waiting for transfers between devices  59.3 us (36%)
  starting transfers between devices  34.9 us (21%)
  blocking collectives  27.2 us (16%)
  other arithmetic  19.2 us (11%)
  between operations  14.2 us (9%)
  local copies, waits for them, and re-layouts  11.1 us (7%)
    psum x1, waiting for transfers between devices, shards(): heat_all, surf_all = lax.psum((heat_part, surf_part), 'ga')  55 us
    all_to_all x1, starting transfers between devices, shards(): lax.all_to_all(state.reshape(2, nblock, per, quarter), 'blk', split_axis=...  18.6 us
    all_to_all x1, starting transfers between devices, shards(): lax.all_to_all(heat_mine.reshape(nblock, per, quarter), 'blk', split_axis...  16.4 us
    all_gather x1, blocking collectives, shards(): lax.all_gather(condensate_optic, 'ga', axis=1, tiled=True)  10.2 us
    all_gather x1, blocking collectives, shards(): lax.all_gather(moved, 'ga', axis=2, tiled=True)  9.11 us
    psum x1, blocking collectives, shards(): heat_all, surf_all = lax.psum((heat_part, surf_part), 'ga')  7.89 us
    reduce_sum x8, other arithmetic, optical_depths(): warming_rate = 0.0625 * jnp.sum(solar_part - emitted, axis=0)  7.2 us
    unnamed x22, local copies, waits for them, and re-layouts  5.36 us
  transfers between devices with their start and end apart: 3, of which 2 were waited for; matrix products, arithmetic and copies ran while one was open for 2% of the time, Pallas kernels for 0%

commit v1 on v0

v1 whole, which is shorter than its diff:
```python
import jax
import jax.numpy as jnp
from jax import lax
from jax.experimental import pallas as pl
from jax.experimental.pallas import tpu as pltpu
from jax.sharding import PartitionSpec as P

F32 = jnp.float32
BF16 = jnp.bfloat16
LOG2E = 1.4426950408889634
MESH = pl.DeviceIdType.MESH


def iota(shape, dim):
    return lax.broadcasted_iota(jnp.int32, shape, dim)


def split3(v):
    hi = v.astype(BF16)
    rest = v - hi.astype(F32)
    mid = rest.astype(BF16)
    lo = (rest - mid.astype(F32)).astype(BF16)
    return hi, mid, lo


def kernel(
    t_ref, w_ref, c_ref, mu_ref, g_ref, op_ref, tp_ref, sw_ref, tw_ref,
    heat_ref, surf_ref,
    scr_c, tx_c, rx_c, tx_g, rx_g, tx_h, rx_h, tx_s, rx_s,
    onehot, t_s, w_s, c_s, prm, acc,
    c_send, c_recv, g_send, g_recv, h_send, h_recv, s_send, s_recv,
):
    b = lax.axis_index("blk")
    a = lax.axis_index("ga")
    b_hi, b_lo = b // 32, b % 32
    mine = b_hi == a

    bar = pltpu.get_barrier_semaphore()

    def greet(dev):
        pl.semaphore_signal(bar, inc=1, device_id=dev, device_id_type=MESH)

    @pl.when(jnp.logical_not(mine))
    def _():
        greet((32 * a + b_lo, a))

    def greet_step(j, carry):
        greet((32 * a + (b_lo + j // 4) % 32, (a + j % 4) % 4))
        return carry

    lax.fori_loop(1, 128, greet_step, 0)
    for k in range(1, 4):
        greet((b, (a + k) % 4))

    scr_c[...] = c_ref[...].astype(F32)
    even = scr_c[pl.ds(0, 128, stride=2), :]
    odd = scr_c[pl.ds(1, 128, stride=2), :]
    mu_b = jnp.broadcast_to(jnp.maximum(mu_ref[...], 0.0), (128, 256))
    row, col = iota((128, 256), 0), iota((128, 256), 1)
    mu_0 = jnp.sum(jnp.where(col == 2 * row, mu_b, 0.0), axis=1, keepdims=True)
    mu_1 = jnp.sum(jnp.where(col == 2 * row + 1, mu_b, 0.0), axis=1, keepdims=True)
    msg = jnp.concatenate([even, odd, jnp.zeros((128, 64), F32)], axis=1)
    lane = iota((128, 128), 1)
    msg = jnp.where(lane == 64, mu_0, jnp.where(lane == 65, mu_1, msg))
    tx_c[:, 0, :] = msg

    grow = jnp.broadcast_to(g_ref[...].astype(F32), (256, 256))
    row, col = iota((256, 256), 0), iota((256, 256), 1)
    gcol = jnp.sum(jnp.where(row == col, grow, 0.0), axis=1, keepdims=True)
    second = jnp.sum(
        jnp.where(jnp.logical_and(grow == gcol, col < row), 1.0, 0.0), axis=1, keepdims=True
    )
    gi = gcol.astype(jnp.int32)
    place = (gi // 32) * 128 + second.astype(jnp.int32) * 32 + gi % 32
    n = iota((256, 512), 1)
    hot = jnp.where((n // 128) * 128 + n % 64 == place, 1.0, 0.0)
    onehot[...] = jnp.where(n % 128 < 64, hot, 0.0).astype(BF16)
    hot = hot.astype(BF16)
    for at, ref in ((0, t_ref), (32, w_ref)):
        moved = lax.dot_general(
            ref[...], hot, (((0,), (0,)), ((), ())), preferred_element_type=F32
        ).astype(BF16)
        for k in range(4):
            tx_g[k, at : at + 32, :] = moved[:, 128 * k : 128 * k + 128]

    prow, plane = iota((16, 128), 0), iota((16, 128), 1)
    tile = jnp.zeros((16, 128), F32)
    for j, ref in enumerate((op_ref, tp_ref, sw_ref, tw_ref)):
        v = ref[...]
        v = jnp.concatenate([v, v], axis=1)
        for s, part in enumerate(split3(v)):
            tile = jnp.where(prow == 3 * j + s, jnp.broadcast_to(part.astype(F32), (16, 128)), tile)
    tile = jnp.where(plane // 64 == a % 2, tile, 0.0).astype(BF16)
    for k in range(4):
        tx_g[k, 64:80, :] = tile

    pl.semaphore_wait(bar, jnp.where(mine, 130, 131))

    def c_copy(to):
        return pltpu.make_async_remote_copy(
            src_ref=tx_c.at[to],
            dst_ref=rx_c.at[a * 32 + b_lo],
            send_sem=c_send,
            recv_sem=c_recv,
            device_id=(to, b_hi),
            device_id_type=MESH,
        )

    def g_copy(k):
        to = (a + k) % 4
        return pltpu.make_async_remote_copy(
            src_ref=tx_g.at[to],
            dst_ref=rx_g.at[a],
            send_sem=g_send,
            recv_sem=g_recv,
            device_id=(b, to),
            device_id_type=MESH,
        )

    for k in range(1, 4):
        g_copy(k).start()

    @pl.when(mine)
    def _():
        pltpu.make_async_copy(tx_c.at[b], rx_c.at[a * 32 + b_lo], c_recv).start()

    @pl.when(jnp.logical_not(mine))
    def _():
        c_copy(b).start()

    def c_step(j, carry):
        c_copy((b + j) % 128).start()
        return carry

    lax.fori_loop(1, 128, c_step, 0)
    rx_g[a] = tx_g[a]

    def await_bytes(ref, sem):
        pltpu.make_async_copy(ref, ref, sem).wait()

    await_bytes(rx_g.at[pl.ds(0, 3)], g_recv)
    for k in range(4):
        t_s[32 * k : 32 * k + 32, :] = rx_g[k, 0:32, :].astype(F32)
        w_s[32 * k : 32 * k + 32, :] = rx_g[k, 32:64, :].astype(F32)
    parts = [rx_g[k, 64:80, :].astype(F32) for k in range(4)]
    parts = jnp.concatenate([parts[0] + parts[1], parts[2] + parts[3]], axis=0)
    m, n = iota((32, 512), 0), iota((32, 512), 1)
    pick = jnp.logical_and(
        m // 16 == (n % 128) // 64,
        jnp.logical_and((m % 16) // 3 == n // 128, m % 16 < 12),
    )
    pick = jnp.where(pick, 1.0, 0.0).astype(BF16)
    spread = lax.dot_general(
        jnp.transpose(parts).astype(BF16), pick, (((1,), (0,)), ((), ())),
        preferred_element_type=F32,
    )
    prm[0] = spread[:, 0:128] * (-1.66 * LOG2E)
    prm[1] = spread[:, 128:256] * LOG2E
    prm[2] = spread[:, 256:384]
    prm[3] = spread[:, 384:512]

    m, n = iota((256, 512), 0), iota((256, 512), 1)
    slot = m % 128
    pick = jnp.logical_and(slot // 32 == n // 128, n % 64 == (m // 128) * 32 + slot % 32)
    pick = jnp.where(pick, 1.0, 0.0).astype(BF16)
    await_bytes(rx_c, c_recv)
    got = jnp.transpose(rx_c[:, 0, :])
    both = jnp.concatenate([got[0:32], got[32:64]], axis=1).astype(BF16)
    cond = lax.dot_general(both, pick, (((1,), (0,)), ((), ())), preferred_element_type=F32)
    for k in range(4):
        c_s[32 * k : 32 * k + 32, :] = cond[:, 128 * k : 128 * k + 128]
    sun = got[64:72]
    lane = iota((1, 128), 1)
    sun = jnp.where(lane % 64 < 32, sun[0:1], pltpu.roll(sun, 32, 1)[1:2])
    sun = jnp.where(lane < 64, jnp.broadcast_to(sun, (8, 128)), 0.0)
    sun = sun + pltpu.roll(sun, 64, 1)

    def h_copy(to):
        return pltpu.make_async_remote_copy(
            src_ref=tx_h.at[to],
            dst_ref=rx_h.at[a],
            send_sem=h_send,
            recv_sem=h_recv,
            device_id=(b, to),
            device_id_type=MESH,
        )

    def level(k, trans):
        t = jnp.broadcast_to(t_s[pl.ds(k, 1), :], (8, 128))
        w = jnp.broadcast_to(w_s[pl.ds(k, 1), :], (8, 128))
        c = jnp.broadcast_to(c_s[pl.ds(k, 1), :], (8, 128))
        q = 1.0 + 0.2 * t
        total = None
        out = []
        for i in range(16):
            rows = slice(8 * i, 8 * i + 8)
            x = w * jnp.exp2(prm[1, rows, :] * t) + c
            e = jnp.exp2(prm[0, rows, :] * x)
            term = (1.0 - e) * (trans[i] - prm[3, rows, :] * q)
            out.append(trans[i] * e)
            total = term if total is None else total + term
        acc[k] = total
        return tuple(out)

    trans = tuple(prm[2, 8 * i : 8 * i + 8, :] * sun for i in range(16))
    for part in range(4):
        trans = lax.fori_loop(32 * part, 32 * part + 32, level, trans, unroll=2)
        heat = 0.0625 * jnp.sum(acc[32 * part : 32 * part + 32], axis=1)
        heat = heat + pltpu.roll(heat, 64, 1)

        @pl.when(a == part)
        def _():
            rx_h[part] = heat

        @pl.when(a != part)
        def _():
            tx_h[part] = heat
            h_copy(part).start()

    surf = trans[0]
    for i in range(1, 16):
        surf = surf + trans[i]
    surf = jnp.sum(surf, axis=0, keepdims=True)
    surf = jnp.broadcast_to(surf, (8, 128))
    surf = surf + pltpu.roll(surf, 64, 1)
    tx_s[0] = surf[0:1]

    def s_copy(j):
        return pltpu.make_async_remote_copy(
            src_ref=tx_s.at[0],
            dst_ref=rx_s.at[b_lo],
            send_sem=s_send,
            recv_sem=s_recv,
            device_id=(32 * a + (b_lo + j) % 32, b_hi),
            device_id_type=MESH,
        )

    @pl.when(mine)
    def _():
        pltpu.make_async_copy(tx_s.at[0], rx_s.at[b_lo], s_recv).start()

    @pl.when(jnp.logical_not(mine))
    def _():
        s_copy(0).start()

    def s_step(j, carry):
        s_copy(j).start()
        return carry

    lax.fori_loop(1, 32, s_step, 0)

    await_bytes(rx_h.at[pl.ds(0, 3)], h_recv)
    heat = jnp.concatenate([rx_h[k] for k in range(4)], axis=1)
    total = None
    for part in split3(heat):
        term = lax.dot_general(
            onehot[...], part, (((1,), (1,)), ((), ())), preferred_element_type=F32
        )
        total = term if total is None else total + term
    heat_ref[...] = total

    await_bytes(rx_s, s_recv)
    got = rx_s[:, 0, :]
    lane, row = iota((32, 128), 1), iota((32, 128), 0)
    first = jnp.sum(jnp.where(lane == b_lo, got, 0.0), axis=1, keepdims=True)
    second = jnp.sum(jnp.where(lane == 32 + b_lo, got, 0.0), axis=1, keepdims=True)
    rows = jnp.where(lane == 2 * row, first, jnp.where(lane == 2 * row + 1, second, 0.0))
    surf_ref[...] = jnp.sum(rows, axis=0, keepdims=True)[:, 0:64]

    await_bytes(tx_g.at[pl.ds(0, 3)], g_send)
    await_bytes(tx_h.at[pl.ds(0, 3)], h_send)

    @pl.when(mine)
    def _():
        await_bytes(tx_c.at[pl.ds(0, 127)], c_send)
        await_bytes(rx_s.at[pl.ds(0, 31)], s_send)

    @pl.when(jnp.logical_not(mine))
    def _():
        await_bytes(tx_c, c_send)
        await_bytes(rx_s, s_send)


def shards(
    thermal_deviation, moisture_mass, condensate_optic, sun_height_factor, group_assignment,
    opacity_factor, thermal_power, sunlight_weights, thermal_weights,
):
    vmem = pl.BlockSpec(memory_space=pltpu.VMEM)
    heating, surface = pl.pallas_call(
        kernel,
        out_shape=(
            jax.ShapeDtypeStruct((256, 32), F32),
            jax.ShapeDtypeStruct((1, 64), F32),
        ),
        in_specs=[vmem] * 9,
        out_specs=(vmem, vmem),
        scratch_shapes=[
            pltpu.VMEM((256, 32), F32),
            pltpu.VMEM((128, 1, 128), F32),
            pltpu.VMEM((128, 1, 128), F32),
            pltpu.VMEM((4, 80, 128), BF16),
            pltpu.VMEM((4, 80, 128), BF16),
            pltpu.VMEM((4, 32, 128), F32),
            pltpu.VMEM((4, 32, 128), F32),
            pltpu.VMEM((1, 1, 128), F32),
            pltpu.VMEM((32, 1, 128), F32),
            pltpu.VMEM((256, 512), BF16),
            pltpu.VMEM((128, 128), F32),
            pltpu.VMEM((128, 128), F32),
            pltpu.VMEM((128, 128), F32),
            pltpu.VMEM((4, 128, 128), F32),
            pltpu.VMEM((128, 8, 128), F32),
        ]
        + [pltpu.SemaphoreType.DMA] * 8,
        compiler_params=pltpu.CompilerParams(
            collective_id=0, has_side_effects=True, vmem_limit_bytes=24 * 1024 * 1024
        ),
    )(
        thermal_deviation,
        moisture_mass,
        condensate_optic,
        sun_height_factor.reshape(1, -1),
        group_assignment.reshape(1, -1),
        opacity_factor.reshape(1, -1),
        thermal_power.reshape(1, -1),
        sunlight_weights.reshape(1, -1),
        thermal_weights.reshape(1, -1),
    )
    return heating, surface.reshape(-1)


def solution(mesh):
    in_specs = (
        P("blk", "ga"), P("blk", "ga"), P("blk", "ga"), P("blk"), P("blk"),
        P("ga"), P("ga"), P("ga"), P("ga"),
    )
    out_specs = (P("blk", "ga"), P(("blk", "ga")))
    return jax.shard_map(shards, mesh=mesh, in_specs=in_specs, out_specs=out_specs, check_vma=False)
```

time: 167 us -> 44.4 us (0.27)
  the two profiles are of different devices: /device:TPU:1 before, /device:TPU:5 now
where the time goes in v1:
time: 44.4 us; the launch traced here: 44.1 us
  Pallas kernels  40 us (90%)
  local copies, waits for them, and re-layouts  3.47 us (8%)
  between operations  0.69 us (2%)
    pallas_call x1, Pallas kernels, shards(): pl.pallas_call(kernel, out_shape=(jax.ShapeDtypeStruct((256, 32), F32), j...  40 us
    unnamed x21, local copies, waits for them, and re-layouts  3.47 us

profile of v1, /device:TPU:5, one launch (start us, length us, event | category | flops | bytes accessed | tf_op | source)
XLA Modules:
  0.0 44.1 jit_solution(16180635683646968627)
XLA Ops:
  0.6 0.0 copy-start.6
  0.6 0.8 %copy.11.t_ref = bf16[256,32]{1,0:T(8,128)(2,1)S(1)} copy(bf16[256,32]{0,1:T(8,128)(2,1)} %param.9) | data formatting | bytes 32768 | tf_op args[0]
  1.5 0.0 copy-done.6
  1.5 0.0 copy-start.7
  1.5 0.1 copy.12.w_ref
  1.6 0.6 %copy-done.7 = bf16[256,32]{0,1:T(8,128)(2,1)S(1)} copy-done((bf16[256,32]{0,1:T(8,128)(2,1)S(1)}, bf16[256,32]{0,1:T(8,128)(2,1)}, u32[]{:S(2)}) %copy-start.7) | copy-done | bytes 16408
  2.2 0.0 copy-start
  2.2 0.0 copy-start.1
  2.2 0.0 copy-start.2
  2.2 0.0 copy-start.3
  2.2 0.0 copy-start.4
  2.2 0.0 copy-start.5
  2.2 0.1 copy.13.c_ref
  2.4 0.5 %copy-done = f32[256]{0:T(256)S(1)} copy-done((f32[256]{0:T(256)S(1)}, f32[256]{0:T(256)}, u32[]{:S(2)}) %copy-start) | copy-done | bytes 1048
  2.9 0.0 copy-done.1
  2.9 0.0 copy-done.2
  2.9 0.0 copy-done.3
  2.9 0.0 copy-done.4
  2.9 0.0 copy-done.5
  2.9 40.0 %shard_map.104 = (f32[256,32]{1,0:T(8,128)S(1)}, f32[1,64]{1,0:T(1,128)S(1)}) custom-call(bf16[256,32]{1,0:T(8,128)(2,1)S(1)} %copy.11.t_ref, bf16[256,32]{1,0:T(8,128)(2,1)S(1)} %copy.12.w_ref, bf16[256,32]{1,0:T(8,128)(2,1)S(1)} %copy.13.c_ref, f32[1,256]{1,0:T(1,128)S(1)} %bitcast.7, s32[1,256]{1,0:T(1,128)S(1)} %bitcast.8, f32[1,64]{1,0:T(1,128)S(1)} %bitcast.9, ...), custom_call_target="tpu_custom_call" | custom-call | tf_op jit(solution)/shard_map/pallas_call | solution.py:289
  42.9 0.7 %copy.14 = f32[256,32]{0,1:T(8,128)} copy(f32[256,32]{1,0:T(8,128)S(1)} %get-tuple-element.6) | data formatting | bytes 65536
  43.6 0.5 %copy.16 = f32[64]{0:T(128)} copy(f32[64]{0:T(128)S(1)} %bitcast.13) | data formatting | bytes 512
Async XLA Ops:
  0.6 0.9 %copy-start.6 = (bf16[256,32]{0,1:T(8,128)(2,1)S(1)}, bf16[256,32]{0,1:T(8,128)(2,1)}, u32[]{:S(2)}) copy-start(bf16[256,32]{0,1:T(8,128)(2,1)} %param.10) | copy-start | bytes 49156
  1.5 0.7 %copy-start.7 = (bf16[256,32]{0,1:T(8,128)(2,1)S(1)}, bf16[256,32]{0,1:T(8,128)(2,1)}, u32[]{:S(2)}) copy-start(bf16[256,32]{0,1:T(8,128)(2,1)} %param.11) | copy-start | bytes 49156
  2.2 0.7 %copy-start = (f32[256]{0:T(256)S(1)}, f32[256]{0:T(256)}, u32[]{:S(2)}) copy-start(f32[256]{0:T(256)} %param.12) | copy-start | bytes 3076
  2.2 0.7 %copy-start.1 = (s32[256]{0:T(256)S(1)}, s32[256]{0:T(256)}, u32[]{:S(2)}) copy-start(s32[256]{0:T(256)} %param.13) | copy-start | bytes 3076
  2.2 0.7 %copy-start.2 = (f32[64]{0:T(128)S(1)}, f32[64]{0:T(128)}, u32[]{:S(2)}) copy-start(f32[64]{0:T(128)} %param.14) | copy-start | bytes 772
  2.2 0.7 %copy-start.3 = (f32[64]{0:T(128)S(1)}, f32[64]{0:T(128)}, u32[]{:S(2)}) copy-start(f32[64]{0:T(128)} %param.15) | copy-start | bytes 772
  2.2 0.7 %copy-start.4 = (f32[64]{0:T(128)S(1)}, f32[64]{0:T(128)}, u32[]{:S(2)}) copy-start(f32[64]{0:T(128)} %param.16) | copy-start | bytes 772
  2.2 0.7 %copy-start.5 = (f32[64]{0:T(128)S(1)}, f32[64]{0:T(128)}, u32[]{:S(2)}) copy-start(f32[64]{0:T(128)} %param.17) | copy-start | bytes 772

commit v2 on v1

v2 whole, which is shorter than its diff:
```python
import jax
import jax.numpy as jnp
from jax import lax
from jax.experimental import pallas as pl
from jax.experimental.pallas import tpu as pltpu
from jax.sharding import PartitionSpec as P

F32 = jnp.float32
BF16 = jnp.bfloat16
LOG2E = 1.4426950408889634
MESH = pl.DeviceIdType.MESH


def iota(shape, dim):
    return lax.broadcasted_iota(jnp.int32, shape, dim)


def split3(v):
    hi = v.astype(BF16)
    rest = v - hi.astype(F32)
    mid = rest.astype(BF16)
    lo = (rest - mid.astype(F32)).astype(BF16)
    return hi, mid, lo


def dot(x, y, dims):
    return lax.dot_general(x, y, (dims, ((), ())), preferred_element_type=F32)


def ones_where(cond):
    return jnp.where(cond, 1.0, 0.0).astype(BF16)


def kernel(
    t_hbm, w_hbm, c_hbm, mu_hbm, g_hbm, op_hbm, tp_hbm, sw_hbm, tw_hbm,
    heat_ref, surf_ref,
    t_in, w_in, c_in, mu_in, g_in, op_in, tp_in, sw_in, tw_in,
    tx_c, rx_c, tx_g, rx_g, tx_h, rx_h, tx_s, rx_s,
    onehot, t_s, w_s, c_s, prm, acc, xs,
    in_sem, c_send, c_recv, g_send, g_recv, h_send, h_recv, s_send, s_recv,
):
    b = lax.axis_index("blk")
    a = lax.axis_index("ga")
    b_hi, b_lo = b >> 5, b & 31
    mine = b_hi == a

    loads = [
        pltpu.make_async_copy(src, dst, in_sem.at[i])
        for i, (src, dst) in enumerate(
            (
                (c_hbm, c_in), (mu_hbm, mu_in), (g_hbm, g_in), (t_hbm, t_in), (w_hbm, w_in),
                (op_hbm, op_in), (tp_hbm, tp_in), (sw_hbm, sw_in), (tw_hbm, tw_in),
            )
        )
    ]
    for load in loads:
        load.start()

    bar = pltpu.get_barrier_semaphore()

    def greet(dev):
        pl.semaphore_signal(bar, inc=1, device_id=dev, device_id_type=MESH)

    for k in range(1, 4):
        greet((b, (a + k) & 3))

    @pl.when(jnp.logical_not(mine))
    def _():
        greet((32 * a + b_lo, a))

    def greet_step(j, carry):
        greet((32 * a + ((b_lo + (j >> 2)) & 31), (a + j) & 3))
        return carry

    lax.fori_loop(1, 128, greet_step, 0, unroll=8)

    loads[0].wait()
    loads[1].wait()
    c_t = c_in[...]
    sun_row = jnp.maximum(mu_in[...], 0.0)
    row, col = iota((16, 512), 0), iota((16, 512), 1)
    sun_two = jnp.broadcast_to(jnp.concatenate([sun_row, sun_row], axis=1), (16, 512))
    sun_tile = jnp.zeros((16, 512), F32)
    for s, part in enumerate(split3(sun_two)):
        sun_tile = jnp.where(row == 3 * (col >> 8) + s, part.astype(F32), sun_tile)
    none = jnp.zeros((32, 256), BF16)
    laid = jnp.concatenate(
        [
            jnp.concatenate([c_t, none], axis=1),
            jnp.concatenate([none, c_t], axis=1),
            sun_tile.astype(BF16),
            jnp.zeros((48, 512), BF16),
        ],
        axis=0,
    )
    row, col = iota((128, 512), 0), iota((128, 512), 1)
    pick = ones_where((col & 255) == 2 * row + (col >> 8))
    tx_c[:, 0, :] = dot(pick, laid, ((1,), (1,)))

    loads[2].wait()
    groups = g_in[...]
    member = groups == iota((128, 256), 0)
    earlier = ones_where(iota((256, 256), 0) < iota((256, 256), 1))
    before = dot(ones_where(member), earlier, ((1,), (0,)))
    second = jnp.sum(jnp.where(member, before, 0.0), axis=0, keepdims=True).astype(jnp.int32)
    place = (groups >> 5) * 128 + second * 32 + (groups & 31)
    n = iota((512, 256), 0)
    hot = ones_where((n & 447) == place)
    onehot[...] = hot
    loads[3].wait()
    loads[4].wait()
    moved = dot(jnp.concatenate([t_in[...], w_in[...]], axis=0), hot, ((1,), (1,))).astype(BF16)
    for k in range(4):
        tx_g[k, 0:64, :] = moved[:, 128 * k : 128 * k + 128]

    for load in loads[5:]:
        load.wait()
    row, lane = iota((16, 128), 0), iota((16, 128), 1)
    tile = jnp.zeros((16, 128), F32)
    for j, ref in enumerate((op_in, tp_in, sw_in, tw_in)):
        v = ref[...]
        v = jnp.broadcast_to(jnp.concatenate([v, v], axis=1), (16, 128))
        for s, part in enumerate(split3(v)):
            tile = jnp.where(row == 3 * j + s, part.astype(F32), tile)
    tile = jnp.where((lane >> 6) == (a & 1), tile, 0.0)
    c_sum = jnp.sum(c_t.astype(F32), axis=0, keepdims=True)
    for k in range(2):
        v = jnp.broadcast_to(c_sum[:, 128 * k : 128 * k + 128], (16, 128))
        full = tile
        for s, part in enumerate(split3(v)):
            full = jnp.where(row == 12 + s, part.astype(F32), full)
        for half in range(2):
            tx_g[2 * k + half, 64:80, :] = full.astype(BF16)

    pl.semaphore_wait(bar, jnp.where(mine, 130, 131))

    def c_copy(to):
        return pltpu.make_async_remote_copy(
            src_ref=tx_c.at[to],
            dst_ref=rx_c.at[a * 32 + b_lo],
            send_sem=c_send,
            recv_sem=c_recv,
            device_id=(to, b_hi),
            device_id_type=MESH,
        )

    def g_copy(k):
        to = (a + k) & 3
        return pltpu.make_async_remote_copy(
            src_ref=tx_g.at[to],
            dst_ref=rx_g.at[a],
            send_sem=g_send,
            recv_sem=g_recv,
            device_id=(b, to),
            device_id_type=MESH,
        )

    for k in range(1, 4):
        g_copy(k).start()

    @pl.when(mine)
    def _():
        pltpu.make_async_copy(tx_c.at[b], rx_c.at[a * 32 + b_lo], c_recv).start()

    @pl.when(jnp.logical_not(mine))
    def _():
        c_copy(b).start()

    def c_step(j, carry):
        c_copy((b + j) & 127).start()
        return carry

    lax.fori_loop(1, 128, c_step, 0, unroll=8)
    rx_g[a] = tx_g[a]

    def await_bytes(ref, sem):
        pltpu.make_async_copy(ref, ref, sem).wait()

    await_bytes(rx_g.at[pl.ds(0, 3)], g_recv)
    for k in range(4):
        t_s[32 * k : 32 * k + 32, :] = rx_g[k, 0:32, :].astype(F32)
        w_s[32 * k : 32 * k + 32, :] = rx_g[k, 32:64, :].astype(F32)
    parts = [rx_g[k, 64:80, :].astype(F32) for k in range(4)]
    parts = [parts[0] + parts[1], parts[2] + parts[3]]
    m, n = iota((32, 512), 0), iota((32, 512), 1)
    pick = jnp.logical_and(
        (m >> 4) == ((n & 127) >> 6),
        jnp.logical_and((m & 15) // 3 == (n >> 7), (m & 15) < 12),
    )
    spread = dot(
        jnp.transpose(jnp.concatenate(parts, axis=0)).astype(BF16), ones_where(pick), ((1,), (0,))
    )
    prm[0] = spread[:, 0:128] * (-1.66 * LOG2E)
    prm[1] = spread[:, 128:256] * LOG2E
    prm[2] = spread[:, 256:384]
    prm[3] = spread[:, 384:512]

    def absorb(k, sums):
        t = jnp.broadcast_to(t_s[pl.ds(k, 1), :], (8, 128))
        w = jnp.broadcast_to(w_s[pl.ds(k, 1), :], (8, 128))
        out = []
        for i in range(16):
            x = w * jnp.exp2(prm[1, 8 * i : 8 * i + 8, :] * t)
            xs[k, 8 * i : 8 * i + 8, :] = x
            out.append(sums[i] + x)
        return tuple(out)

    sums = lax.fori_loop(
        0, 128, absorb, tuple(jnp.zeros((8, 128), F32) for i in range(16)), unroll=2
    )

    sums = jnp.transpose(jnp.concatenate(sums, axis=0))
    for k in range(4):
        tx_s[:, k, :] = sums[32 * k : 32 * k + 32]

    def s_copy(j):
        to = (b_lo + j) & 31
        return pltpu.make_async_remote_copy(
            src_ref=tx_s.at[to],
            dst_ref=rx_s.at[b_lo],
            send_sem=s_send,
            recv_sem=s_recv,
            device_id=(32 * a + to, b_hi),
            device_id_type=MESH,
        )

    @pl.when(mine)
    def _():
        pltpu.make_async_copy(tx_s.at[b_lo], rx_s.at[b_lo], s_recv).start()

    @pl.when(jnp.logical_not(mine))
    def _():
        s_copy(0).start()

    def s_step(j, carry):
        s_copy(j).start()
        return carry

    lax.fori_loop(1, 32, s_step, 0, unroll=4)

    m, n = iota((256, 512), 0), iota((256, 512), 1)
    slot = m & 127
    pick = jnp.logical_and((slot >> 5) == (n >> 7), (n & 63) == (m >> 7) * 32 + (slot & 31))
    pick = ones_where(pick)
    await_bytes(rx_c, c_recv)
    got = jnp.transpose(rx_c[:, 0, :])
    both = jnp.concatenate([got[0:32], got[32:64]], axis=1).astype(BF16)
    cond = dot(both, pick, ((1,), (0,)))
    for k in range(4):
        c_s[32 * k : 32 * k + 32, :] = cond[:, 128 * k : 128 * k + 128]
    sun = got[64:72]
    first = sun[0:1] + sun[1:2] + sun[2:3]
    second = jnp.broadcast_to(sun[3:4] + sun[4:5] + sun[5:6], (8, 128))
    lane = iota((8, 128), 1)
    sun = jnp.where((lane & 63) < 32, jnp.broadcast_to(first, (8, 128)), pltpu.roll(second, 32, 1))
    sun = jnp.where(lane < 64, sun, 0.0)
    sun = sun + pltpu.roll(sun, 64, 1)

    def h_copy(to):
        return pltpu.make_async_remote_copy(
            src_ref=tx_h.at[to],
            dst_ref=rx_h.at[a],
            send_sem=h_send,
            recv_sem=h_recv,
            device_id=(b, to),
            device_id_type=MESH,
        )

    def level(k, trans):
        q = jnp.broadcast_to(1.0 + 0.2 * t_s[pl.ds(k, 1), :], (8, 128))
        c = jnp.broadcast_to(c_s[pl.ds(k, 1), :], (8, 128))
        total = None
        out = []
        for i in range(16):
            rows = slice(8 * i, 8 * i + 8)
            e = jnp.exp2(prm[0, rows, :] * (xs[k, rows, :] + c))
            term = (1.0 - e) * (trans[i] - prm[3, rows, :] * q)
            out.append(trans[i] * e)
            total = term if total is None else total + term
        acc[k] = total
        return tuple(out)

    trans = tuple(prm[2, 8 * i : 8 * i + 8, :] * sun for i in range(16))
    for part in range(4):
        trans = lax.fori_loop(32 * part, 32 * part + 32, level, trans, unroll=2)
        heat = 0.0625 * jnp.sum(acc[32 * part : 32 * part + 32], axis=1)
        heat = heat + pltpu.roll(heat, 64, 1)

        @pl.when(a == part)
        def _():
            rx_h[part] = heat

        @pl.when(a != part)
        def _():
            tx_h[part] = heat
            h_copy(part).start()

    await_bytes(rx_s, s_recv)
    lane, row = iota((32, 128), 1), iota((32, 128), 0)
    c_all = jnp.broadcast_to(
        jnp.sum(parts[0][12:15] + parts[1][12:15], axis=0, keepdims=True), (32, 128)
    )
    mu_all = jnp.broadcast_to(mu_in[...], (32, 256))
    lane2, row2 = iota((32, 256), 1), iota((32, 256), 0)
    rows = None
    for r in range(2):
        at = 2 * row + r
        c_col = jnp.sum(jnp.where(lane == (a & 1) * 64 + at, c_all, 0.0), axis=1, keepdims=True)
        mu_col = jnp.sum(
            jnp.where(lane2 == a * 64 + 2 * row2 + r, mu_all, 0.0), axis=1, keepdims=True
        )
        flux = None
        for half in range(2):
            par = parts[half]
            factor = jnp.sum(par[0:3], axis=0, keepdims=True) * (-1.66 * LOG2E)
            weight = jnp.sum(par[6:9], axis=0, keepdims=True)
            term = weight * jnp.exp2(factor * (rx_s[:, 2 * half + r, :] + c_col))
            flux = term if flux is None else flux + term
        flux = jnp.sum(flux, axis=1, keepdims=True) * jnp.maximum(mu_col, 0.0)
        flux = jnp.where(lane == at, flux, 0.0)
        rows = flux if rows is None else rows + flux
    surf_ref[...] = jnp.sum(rows, axis=0, keepdims=True)[:, 0:64]

    await_bytes(rx_h.at[pl.ds(0, 3)], h_recv)
    heat = jnp.concatenate([rx_h[k] for k in range(4)], axis=1)
    heat = jnp.where((iota((32, 512), 1) & 127) < 64, heat, 0.0)
    heat = dot(jnp.concatenate(split3(heat), axis=0), onehot[...], ((1,), (0,)))
    heat_ref[...] = heat[0:32] + heat[32:64] + heat[64:96]

    await_bytes(tx_g.at[pl.ds(0, 3)], g_send)
    await_bytes(tx_h.at[pl.ds(0, 3)], h_send)

    @pl.when(mine)
    def _():
        await_bytes(tx_c.at[pl.ds(0, 127)], c_send)
        await_bytes(tx_s.at[pl.ds(0, 31)], s_send)

    @pl.when(jnp.logical_not(mine))
    def _():
        await_bytes(tx_c, c_send)
        await_bytes(tx_s, s_send)


def shards(
    thermal_deviation, moisture_mass, condensate_optic, sun_height_factor, group_assignment,
    opacity_factor, thermal_power, sunlight_weights, thermal_weights,
):
    vmem = pl.BlockSpec(memory_space=pltpu.VMEM)
    heating, surface = pl.pallas_call(
        kernel,
        out_shape=(
            jax.ShapeDtypeStruct((32, 256), F32),
            jax.ShapeDtypeStruct((1, 64), F32),
        ),
        in_specs=[pl.BlockSpec(memory_space=pltpu.HBM)] * 9,
        out_specs=(vmem, vmem),
        scratch_shapes=[
            pltpu.VMEM((32, 256), BF16),
            pltpu.VMEM((32, 256), BF16),
            pltpu.VMEM((32, 256), BF16),
            pltpu.VMEM((1, 256), F32),
            pltpu.VMEM((1, 256), jnp.int32),
            pltpu.VMEM((1, 64), F32),
            pltpu.VMEM((1, 64), F32),
            pltpu.VMEM((1, 64), F32),
            pltpu.VMEM((1, 64), F32),
            pltpu.VMEM((128, 1, 128), F32),
            pltpu.VMEM((128, 1, 128), F32),
            pltpu.VMEM((4, 80, 128), BF16),
            pltpu.VMEM((4, 80, 128), BF16),
            pltpu.VMEM((4, 32, 128), F32),
            pltpu.VMEM((4, 32, 128), F32),
            pltpu.VMEM((32, 4, 128), F32),
            pltpu.VMEM((32, 4, 128), F32),
            pltpu.VMEM((512, 256), BF16),
            pltpu.VMEM((128, 128), F32),
            pltpu.VMEM((128, 128), F32),
            pltpu.VMEM((128, 128), F32),
            pltpu.VMEM((4, 128, 128), F32),
            pltpu.VMEM((128, 8, 128), F32),
            pltpu.VMEM((128, 128, 128), F32),
            pltpu.SemaphoreType.DMA((9,)),
        ]
        + [pltpu.SemaphoreType.DMA] * 8,
        compiler_params=pltpu.CompilerParams(
            collective_id=0, has_side_effects=True, vmem_limit_bytes=60 * 1024 * 1024
        ),
    )(
        thermal_deviation.T,
        moisture_mass.T,
        condensate_optic.T,
        sun_height_factor.reshape(1, -1),
        group_assignment.reshape(1, -1),
        opacity_factor.reshape(1, -1),
        thermal_power.reshape(1, -1),
        sunlight_weights.reshape(1, -1),
        thermal_weights.reshape(1, -1),
    )
    return heating.T, surface.reshape(-1)


def solution(mesh):
    in_specs = (
        P("blk", "ga"), P("blk", "ga"), P("blk", "ga"), P("blk"), P("blk"),
        P("ga"), P("ga"), P("ga"), P("ga"),
    )
    out_specs = (P("blk", "ga"), P(("blk", "ga")))
    return jax.shard_map(shards, mesh=mesh, in_specs=in_specs, out_specs=out_specs, check_vma=False)
```

time: 44.4 us -> 35.1 us (0.79)
  the two profiles are of different devices: /device:TPU:5 before, /device:TPU:6 now
where the time goes in v2:
time: 35.1 us; the launch traced here: 34.9 us
  Pallas kernels  32.4 us (92%)
  local copies, waits for them, and re-layouts  1.89 us (5%)
  between operations  0.65 us (2%)
    pallas_call x1, Pallas kernels, shards(): pl.pallas_call(kernel, out_shape=(jax.ShapeDtypeStruct((32, 256), F32), j...  32.4 us
    unnamed x4, local copies, waits for them, and re-layouts  1.89 us

profile of v2, /device:TPU:6, one launch (start us, length us, event | category | flops | bytes accessed | tf_op | source)
XLA Modules:
  0.0 34.9 jit_solution(18145233138316861000)
XLA Ops:
  0.6 32.4 %shard_map.104 = (f32[32,256]{1,0:T(8,128)}, f32[1,64]{1,0:T(1,128)}) custom-call(bf16[32,256]{1,0:T(8,128)(2,1)} %bitcast.12, bf16[32,256]{1,0:T(8,128)(2,1)} %bitcast.13, bf16[32,256]{1,0:T(8,128)(2,1)} %bitcast.14, f32[1,256]{1,0:T(1,128)} %bitcast.15, s32[1,256]{1,0:T(1,128)} %bitcast.16, f32[1,64]{1,0:T(1,128)} %bitcast.17, f32[1,64]{1,0:T(1,128)} %bitcast.18, ...), custom_call_target="tpu_custom_call" | custom-call | tf_op jit(solution)/shard_map/pallas_call | solution.py:349
  33.0 0.0 copy-start
  33.0 1.4 %copy.13 = f32[256,32]{0,1:T(8,128)} copy(f32[256,32]{0,1:T(8,128)} %bitcast.11) | data formatting | bytes 65536
  34.4 0.0 copy-done
  34.4 0.5 %copy.14 = f32[64]{0:T(128)} copy(f32[64]{0:T(128)S(1)} %bitcast.21) | data formatting | bytes 512
Async XLA Ops:
  33.0 1.4 %copy-start = (f32[1,64]{1,0:T(1,128)S(1)}, f32[1,64]{1,0:T(1,128)}, u32[]{:S(2)}) copy-start(f32[1,64]{1,0:T(1,128)} %get-tuple-element.5) | copy-start | bytes 772

commit v3 on v2

--- a/solution.py
+++ b/solution.py
@@ -7,6 +7,7 @@
 
 F32 = jnp.float32
 BF16 = jnp.bfloat16
+UNROLL = 8
 LOG2E = 1.4426950408889634
 MESH = pl.DeviceIdType.MESH
 
@@ -195,19 +196,20 @@
     prm[2] = spread[:, 256:384]
     prm[3] = spread[:, 384:512]
 
+    power = [prm[1, 8 * i : 8 * i + 8, :] for i in range(16)]
+
     def absorb(k, sums):
-        t = jnp.broadcast_to(t_s[pl.ds(k, 1), :], (8, 128))
-        w = jnp.broadcast_to(w_s[pl.ds(k, 1), :], (8, 128))
-        out = []
-        for i in range(16):
-            x = w * jnp.exp2(prm[1, 8 * i : 8 * i + 8, :] * t)
-            xs[k, 8 * i : 8 * i + 8, :] = x
-            out.append(sums[i] + x)
-        return tuple(out)
-
-    sums = lax.fori_loop(
-        0, 128, absorb, tuple(jnp.zeros((8, 128), F32) for i in range(16)), unroll=2
-    )
+        sums = list(sums)
+        rows_t = [jnp.broadcast_to(t_s[pl.ds(4 * k + u, 1), :], (8, 128)) for u in range(4)]
+        rows_w = [jnp.broadcast_to(w_s[pl.ds(4 * k + u, 1), :], (8, 128)) for u in range(4)]
+        for u in range(4):
+            for i in range(16):
+                x = rows_w[u] * jnp.exp2(power[i] * rows_t[u])
+                xs[4 * k + u, 8 * i : 8 * i + 8, :] = x
+                sums[i] = sums[i] + x
+        return tuple(sums)
+
+    sums = lax.fori_loop(0, 32, absorb, tuple(jnp.zeros((8, 128), F32) for i in range(16)))
 
     sums = jnp.transpose(jnp.concatenate(sums, axis=0))
     for k in range(4):
@@ -266,24 +268,31 @@
             device_id_type=MESH,
         )
 
-    def level(k, trans):
-        q = jnp.broadcast_to(1.0 + 0.2 * t_s[pl.ds(k, 1), :], (8, 128))
-        c = jnp.broadcast_to(c_s[pl.ds(k, 1), :], (8, 128))
-        total = None
-        out = []
-        for i in range(16):
-            rows = slice(8 * i, 8 * i + 8)
-            e = jnp.exp2(prm[0, rows, :] * (xs[k, rows, :] + c))
-            term = (1.0 - e) * (trans[i] - prm[3, rows, :] * q)
-            out.append(trans[i] * e)
-            total = term if total is None else total + term
-        acc[k] = total
-        return tuple(out)
+    def levels(first, trans):
+        rows_q = [
+            jnp.broadcast_to(1.0 + 0.2 * t_s[pl.ds(first + u, 1), :], (8, 128)) for u in range(UNROLL)
+        ]
+        rows_c = [jnp.broadcast_to(c_s[pl.ds(first + u, 1), :], (8, 128)) for u in range(UNROLL)]
+        totals = [None] * UNROLL
+        trans = list(trans)
+        for u in range(UNROLL):
+            for i in range(16):
+                rows = slice(8 * i, 8 * i + 8)
+                e = jnp.exp2(prm[0, rows, :] * (xs[first + u, rows, :] + rows_c[u]))
+                term = (1.0 - e) * (trans[i] - prm[3, rows, :] * rows_q[u])
+                trans[i] = trans[i] * e
+                totals[u] = term if i == 0 else totals[u] + term
+        for u in range(UNROLL):
+            acc[first + u] = totals[u]
+        return tuple(trans)
 
     trans = tuple(prm[2, 8 * i : 8 * i + 8, :] * sun for i in range(16))
-    for part in range(4):
-        trans = lax.fori_loop(32 * part, 32 * part + 32, level, trans, unroll=2)
-        heat = 0.0625 * jnp.sum(acc[32 * part : 32 * part + 32], axis=1)
+    def quarter(part, trans):
+        first = pl.multiple_of(32 * part, 32)
+        trans = lax.fori_loop(
+            0, 32 // UNROLL, lambda k, v: levels(first + UNROLL * k, v), trans
+        )
+        heat = 0.0625 * jnp.sum(acc[pl.ds(first, 32)], axis=1)
         heat = heat + pltpu.roll(heat, 64, 1)
 
         @pl.when(a == part)
@@ -294,6 +303,10 @@
         def _():
             tx_h[part] = heat
             h_copy(part).start()
+
+        return trans
+
+    lax.fori_loop(0, 4, quarter, trans)
 
     await_bytes(rx_s, s_recv)
     lane, row = iota((32, 128), 1), iota((32, 128), 0)
@@ -339,6 +352,17 @@
     def _():
         await_bytes(tx_c, c_send)
         await_bytes(tx_s, s_send)
+
+
+def place(heat_in, surf_in, heat_out, surf_out, sem):
+    copies = [
+        pltpu.make_async_copy(heat_in, heat_out, sem.at[0]),
+        pltpu.make_async_copy(surf_in, surf_out, sem.at[1]),
+    ]
+    for copy in copies:
+        copy.start()
+    for copy in copies:
+        copy.wait()
 
 
 def shards(
@@ -383,19 +407,34 @@
         ]
         + [pltpu.SemaphoreType.DMA] * 8,
         compiler_params=pltpu.CompilerParams(
-            collective_id=0, has_side_effects=True, vmem_limit_bytes=60 * 1024 * 1024
+            collective_id=0, has_side_effects=True, vmem_limit_bytes=32 * 1024 * 1024
         ),
     )(
-        thermal_deviation.T,
-        moisture_mass.T,
-        condensate_optic.T,
-        sun_height_factor.reshape(1, -1),
-        group_assignment.reshape(1, -1),
-        opacity_factor.reshape(1, -1),
-        thermal_power.reshape(1, -1),
-        sunlight_weights.reshape(1, -1),
-        thermal_weights.reshape(1, -1),
-    )
+        *(
+            pltpu.with_memory_space_constraint(v, pltpu.HBM)
+            for v in (
+                thermal_deviation.T,
+                moisture_mass.T,
+                condensate_optic.T,
+                sun_height_factor.reshape(1, -1),
+                group_assignment.reshape(1, -1),
+                opacity_factor.reshape(1, -1),
+                thermal_power.reshape(1, -1),
+                sunlight_weights.reshape(1, -1),
+                thermal_weights.reshape(1, -1),
+            )
+        )
+    )
+    heating, surface = pl.pallas_call(
+        place,
+        out_shape=(
+            jax.ShapeDtypeStruct((32, 256), F32),
+            jax.ShapeDtypeStruct((1, 64), F32),
+        ),
+        in_specs=[vmem] * 2,
+        out_specs=[pl.BlockSpec(memory_space=pltpu.HBM)] * 2,
+        scratch_shapes=[pltpu.SemaphoreType.DMA((2,))],
+    )(*(pltpu.with_memory_space_constraint(v, pltpu.VMEM) for v in (heating, surface)))
     return heating.T, surface.reshape(-1)
 
 

time: 35.1 us -> 32.8 us (0.934)
  local copies, waits for them, and re-layouts: 1.89 us -> 0 us
  Pallas kernels: 32.4 us -> 32 us
    unnamed x4 -> x0, local copies, waits for them, and re-layouts: 1.89 us -> none
    pallas_call x1, Pallas kernels: 32.4 us -> 31.4 us  [shards(): pl.pallas_call(kernel, out_shape=(jax.ShapeDtypeStruct((32, 256), F32), j...]
    pallas_call x0 -> x1, Pallas kernels: none -> 0.64 us  [shards(): pl.pallas_call(place, out_shape=(jax.ShapeDtypeStruct((32, 256), F32), ja...]
where the time goes in v3:
time: 32.8 us; the launch traced here: 32.7 us
  Pallas kernels  32 us (98%)
  between operations  0.64 us (2%)
    pallas_call x1, Pallas kernels, shards(): pl.pallas_call(kernel, out_shape=(jax.ShapeDtypeStruct((32, 256), F32), j...  31.4 us

profile of v3, /device:TPU:6, one launch (start us, length us, event | category | flops | bytes accessed | tf_op | source)
XLA Modules:
  0.0 32.7 jit_solution(7936439703157995087)
XLA Ops:
  0.6 31.4 %shard_map.104 = (f32[32,256]{1,0:T(8,128)S(1)}, f32[1,64]{1,0:T(1,128)S(1)}) custom-call(bf16[32,256]{1,0:T(8,128)(2,1)} %bitcast.11, bf16[32,256]{1,0:T(8,128)(2,1)} %bitcast.12, bf16[32,256]{1,0:T(8,128)(2,1)} %bitcast.13, f32[1,256]{1,0:T(1,128)} %bitcast.14, s32[1,256]{1,0:T(1,128)} %bitcast.15, f32[1,64]{1,0:T(1,128)} %bitcast.16, f32[1,64]{1,0:T(1,128)} %bitcast.17, ...), custom_call_target="tpu_custom_call" | custom-call | tf_op jit(solution)/shard_map/pallas_call | solution.py:373
  32.0 0.6 %shard_map.105 = (f32[32,256]{1,0:T(8,128)}, f32[1,64]{1,0:T(1,128)}) custom-call(f32[32,256]{1,0:T(8,128)S(1)} %get-tuple-element.6.heat_in, f32[1,64]{1,0:T(1,128)S(1)} %get-tuple-element.7.surf_in), custom_call_target="tpu_custom_call" | custom-call | tf_op jit(solution)/shard_map/pallas_call | solution.py:428

commit v4 on v3

--- a/solution.py
+++ b/solution.py
@@ -32,18 +32,36 @@
     return jnp.where(cond, 1.0, 0.0).astype(BF16)
 
 
+EARLY, LATE = 72, 56
+
+
+def is_late(blk):
+    return jnp.logical_or(blk >= 96, jnp.logical_and(blk >= 64, (blk & 15) >= 4))
+
+
+def early_blk(j):
+    return jnp.where(j >= 68, j + 12, j)
+
+
+def late_blk(j):
+    return jnp.where(j >= 12, j + 72, j + 68)
+
+
 def kernel(
     t_hbm, w_hbm, c_hbm, mu_hbm, g_hbm, op_hbm, tp_hbm, sw_hbm, tw_hbm,
     heat_ref, surf_ref,
     t_in, w_in, c_in, mu_in, g_in, op_in, tp_in, sw_in, tw_in,
     tx_c, rx_c, tx_g, rx_g, tx_h, rx_h, tx_s, rx_s,
     onehot, t_s, w_s, c_s, prm, acc, xs,
-    in_sem, c_send, c_recv, g_send, g_recv, h_send, h_recv, s_send, s_recv,
+    in_sem, c_send, c_recv, g_send, g_recv, h_send, h_recv, s_send, s_recv, pair_sem,
 ):
     b = lax.axis_index("blk")
     a = lax.axis_index("ga")
     b_hi, b_lo = b >> 5, b & 31
     mine = b_hi == a
+    core = b & 1
+    late = is_late(b)
+    sibling = (b ^ 1, a)
 
     loads = [
         pltpu.make_async_copy(src, dst, in_sem.at[i])
@@ -62,18 +80,24 @@
     def greet(dev):
         pl.semaphore_signal(bar, inc=1, device_id=dev, device_id_type=MESH)
 
+    greet(sibling)
     for k in range(1, 4):
-        greet((b, (a + k) & 3))
-
-    @pl.when(jnp.logical_not(mine))
-    def _():
-        greet((32 * a + b_lo, a))
-
-    def greet_step(j, carry):
-        greet((32 * a + ((b_lo + (j >> 2)) & 31), (a + j) & 3))
+        greet((b & 126, (a + k) & 3))
+    told = jnp.where(late, 1, 0)
+    told_self = jnp.logical_and(mine, core == told)
+
+    def announce(j):
+        greet((32 * a + ((b_lo + (j >> 2) * 2) & 30) + told, (a + j) & 3))
+
+    @pl.when(jnp.logical_not(told_self))
+    def _():
+        announce(0)
+
+    def announce_step(j, carry):
+        announce(j)
         return carry
 
-    lax.fori_loop(1, 128, greet_step, 0, unroll=8)
+    lax.fori_loop(1, 64, announce_step, 0, unroll=7)
 
     loads[0].wait()
     loads[1].wait()
@@ -133,7 +157,16 @@
         for half in range(2):
             tx_g[2 * k + half, 64:80, :] = full.astype(BF16)
 
-    pl.semaphore_wait(bar, jnp.where(mine, 130, 131))
+    self_counted = jnp.where(told_self, 1, 0)
+
+    @pl.when(core == 0)
+    def _():
+        pl.semaphore_wait(bar, EARLY + 7 - self_counted)
+        pl.semaphore_signal(pair_sem, inc=1, device_id=sibling, device_id_type=MESH)
+
+    @pl.when(core == 1)
+    def _():
+        pl.semaphore_wait(pair_sem, 1)
 
     def c_copy(to):
         return pltpu.make_async_remote_copy(
@@ -163,15 +196,26 @@
     def _():
         pltpu.make_async_copy(tx_c.at[b], rx_c.at[a * 32 + b_lo], c_recv).start()
 
-    @pl.when(jnp.logical_not(mine))
-    def _():
-        c_copy(b).start()
-
-    def c_step(j, carry):
-        c_copy((b + j) & 127).start()
+    early_first = jnp.where(late, (b * 9) >> 4, jnp.where(b >= 68, b - 12, b))
+    late_first = jnp.where(late, jnp.where(b >= 84, b - 72, b - 68), (b * 7) >> 4)
+
+    def early_to(j):
+        j = early_first + j
+        return early_blk(jnp.where(j >= EARLY, j - EARLY, j))
+
+    def late_to(j):
+        j = late_first + j
+        return late_blk(jnp.where(j >= LATE, j - LATE, j))
+
+    @pl.when(jnp.logical_not(jnp.logical_and(mine, jnp.logical_not(late))))
+    def _():
+        c_copy(early_to(0)).start()
+
+    def early_step(j, carry):
+        c_copy(early_to(j)).start()
         return carry
 
-    lax.fori_loop(1, 128, c_step, 0, unroll=8)
+    lax.fori_loop(1, EARLY, early_step, 0, unroll=8)
     rx_g[a] = tx_g[a]
 
     def await_bytes(ref, sem):
@@ -215,30 +259,56 @@
     for k in range(4):
         tx_s[:, k, :] = sums[32 * k : 32 * k + 32]
 
-    def s_copy(j):
-        to = (b_lo + j) & 31
-        return pltpu.make_async_remote_copy(
-            src_ref=tx_s.at[to],
-            dst_ref=rx_s.at[b_lo],
-            send_sem=s_send,
-            recv_sem=s_recv,
-            device_id=(32 * a + to, b_hi),
-            device_id_type=MESH,
-        )
-
     @pl.when(mine)
     def _():
         pltpu.make_async_copy(tx_s.at[b_lo], rx_s.at[b_lo], s_recv).start()
 
-    @pl.when(jnp.logical_not(mine))
-    def _():
-        s_copy(0).start()
-
-    def s_step(j, carry):
-        s_copy(j).start()
+    def s_sends(to_late):
+        def step(j, carry):
+            to = (b_lo + j) & 31
+            wanted = is_late(32 * a + to) == to_late
+
+            @pl.when(jnp.logical_and(wanted, jnp.logical_not(jnp.logical_and(mine, j == 0))))
+            def _():
+                pltpu.make_async_remote_copy(
+                    src_ref=tx_s.at[to],
+                    dst_ref=rx_s.at[b_lo],
+                    send_sem=s_send,
+                    recv_sem=s_recv,
+                    device_id=(32 * a + to, b_hi),
+                    device_id_type=MESH,
+                ).start()
+
+            return carry
+
+        lax.fori_loop(0, 32, step, 0)
+
+    @pl.when(a < 3)
+    def _():
+        s_sends(False)
+
+    @pl.when(core == 0)
+    def _():
+        pl.semaphore_wait(pair_sem, 1)
+
+    @pl.when(core == 1)
+    def _():
+        pl.semaphore_wait(bar, LATE + 1 - self_counted)
+        pl.semaphore_signal(pair_sem, inc=1, device_id=sibling, device_id_type=MESH)
+
+    @pl.when(jnp.logical_not(jnp.logical_and(mine, late)))
+    def _():
+        c_copy(late_to(0)).start()
+
+    def late_step(j, carry):
+        c_copy(late_to(j)).start()
         return carry
 
-    lax.fori_loop(1, 32, s_step, 0, unroll=4)
+    lax.fori_loop(1, LATE, late_step, 0, unroll=5)
+
+    @pl.when(a >= 2)
+    def _():
+        s_sends(True)
 
     m, n = iota((256, 512), 0), iota((256, 512), 1)
     slot = m & 127
@@ -405,7 +475,8 @@
             pltpu.VMEM((128, 128, 128), F32),
             pltpu.SemaphoreType.DMA((9,)),
         ]
-        + [pltpu.SemaphoreType.DMA] * 8,
+        + [pltpu.SemaphoreType.DMA] * 8
+        + [pltpu.SemaphoreType.REGULAR],
         compiler_params=pltpu.CompilerParams(
             collective_id=0, has_side_effects=True, vmem_limit_bytes=32 * 1024 * 1024
         ),

time: 32.8 us -> 30.4 us (0.927)
  the two profiles are of different devices: /device:TPU:6 before, /device:TPU:398 now
where the time goes in v4:
time: 30.4 us; the launch traced here: 30.3 us
  Pallas kernels  29.7 us (98%)
  between operations  0.64 us (2%)
    pallas_call x1, Pallas kernels, shards(): pl.pallas_call(kernel, out_shape=(jax.ShapeDtypeStruct((32, 256), F32), j...  29 us
    pallas_call x1, Pallas kernels, shards(): pl.pallas_call(place, out_shape=(jax.ShapeDtypeStruct((32, 256), F32), ja...  0.64 us

profile of v4, /device:TPU:398, one launch (start us, length us, event | category | flops | bytes accessed | tf_op | source)
XLA Modules:
  0.0 30.3 jit_solution(8709332828119966975)
XLA Ops:
  0.6 29.0 %shard_map.104 = (f32[32,256]{1,0:T(8,128)S(1)}, f32[1,64]{1,0:T(1,128)S(1)}) custom-call(bf16[32,256]{1,0:T(8,128)(2,1)} %bitcast.11, bf16[32,256]{1,0:T(8,128)(2,1)} %bitcast.12, bf16[32,256]{1,0:T(8,128)(2,1)} %bitcast.13, f32[1,256]{1,0:T(1,128)} %bitcast.14, s32[1,256]{1,0:T(1,128)} %bitcast.15, f32[1,64]{1,0:T(1,128)} %bitcast.16, f32[1,64]{1,0:T(1,128)} %bitcast.17, ...), custom_call_target="tpu_custom_call" | custom-call | tf_op jit(solution)/shard_map/pallas_call | solution.py:443
  29.7 0.6 %shard_map.105 = (f32[32,256]{1,0:T(8,128)}, f32[1,64]{1,0:T(1,128)}) custom-call(f32[32,256]{1,0:T(8,128)S(1)} %get-tuple-element.6.heat_in, f32[1,64]{1,0:T(1,128)S(1)} %get-tuple-element.7.surf_in), custom_call_target="tpu_custom_call" | custom-call | tf_op jit(solution)/shard_map/pallas_call | solution.py:499

commit v5 on v4

--- a/solution.py
+++ b/solution.py
@@ -39,21 +39,13 @@
     return jnp.logical_or(blk >= 96, jnp.logical_and(blk >= 64, (blk & 15) >= 4))
 
 
-def early_blk(j):
-    return jnp.where(j >= 68, j + 12, j)
-
-
-def late_blk(j):
-    return jnp.where(j >= 12, j + 72, j + 68)
-
-
 def kernel(
     t_hbm, w_hbm, c_hbm, mu_hbm, g_hbm, op_hbm, tp_hbm, sw_hbm, tw_hbm,
     heat_ref, surf_ref,
     t_in, w_in, c_in, mu_in, g_in, op_in, tp_in, sw_in, tw_in,
     tx_c, rx_c, tx_g, rx_g, tx_h, rx_h, tx_s, rx_s,
-    onehot, t_s, w_s, c_s, prm, acc, xs,
-    in_sem, c_send, c_recv, g_send, g_recv, h_send, h_recv, s_send, s_recv, pair_sem,
+    onehot, t_s, w_s, c_s, c_above, prm, acc, xs, emit, above,
+    in_sem, c_send, c_recv, g_send, g_recv, h_send, h_recv, s_send_sem, s_recv, pair_sem,
 ):
     b = lax.axis_index("blk")
     a = lax.axis_index("ga")
@@ -87,7 +79,7 @@
     told_self = jnp.logical_and(mine, core == told)
 
     def announce(j):
-        greet((32 * a + ((b_lo + (j >> 2) * 2) & 30) + told, (a + j) & 3))
+        greet((32 * a + told + ((2 * (j >> 2)) ^ (b_lo & 30)), (a ^ j) & 3))
 
     @pl.when(jnp.logical_not(told_self))
     def _():
@@ -97,7 +89,7 @@
         announce(j)
         return carry
 
-    lax.fori_loop(1, 64, announce_step, 0, unroll=7)
+    lax.fori_loop(1, 64, announce_step, 0, unroll=9)
 
     loads[0].wait()
     loads[1].wait()
@@ -196,26 +188,25 @@
     def _():
         pltpu.make_async_copy(tx_c.at[b], rx_c.at[a * 32 + b_lo], c_recv).start()
 
-    early_first = jnp.where(late, (b * 9) >> 4, jnp.where(b >= 68, b - 12, b))
-    late_first = jnp.where(late, jnp.where(b >= 84, b - 72, b - 68), (b * 7) >> 4)
-
-    def early_to(j):
-        j = early_first + j
-        return early_blk(jnp.where(j >= EARLY, j - EARLY, j))
-
-    def late_to(j):
-        j = late_first + j
-        return late_blk(jnp.where(j >= LATE, j - LATE, j))
-
-    @pl.when(jnp.logical_not(jnp.logical_and(mine, jnp.logical_not(late))))
-    def _():
-        c_copy(early_to(0)).start()
+    @pl.when(jnp.logical_not(jnp.logical_and(mine, b < 64)))
+    def _():
+        c_copy(b & 63).start()
 
     def early_step(j, carry):
-        c_copy(early_to(j)).start()
+        c_copy(j ^ (b & 63)).start()
         return carry
 
-    lax.fori_loop(1, EARLY, early_step, 0, unroll=8)
+    lax.fori_loop(1, 64, early_step, 0, unroll=9)
+
+    def between(members):
+        for j in members:
+            to = (64 + j) ^ (b & 19)
+
+            @pl.when(jnp.logical_not(jnp.logical_and(mine, b == to)))
+            def _():
+                c_copy(to).start()
+
+    between([j for j in range(32) if j & 15 < 4])
     rx_g[a] = tx_g[a]
 
     def await_bytes(ref, sem):
@@ -253,7 +244,11 @@
                 sums[i] = sums[i] + x
         return tuple(sums)
 
-    sums = lax.fori_loop(0, 32, absorb, tuple(jnp.zeros((8, 128), F32) for i in range(16)))
+    sums = tuple(jnp.zeros((8, 128), F32) for i in range(16))
+    for k in range(4):
+        for i in range(16):
+            above[k, 8 * i : 8 * i + 8, :] = sums[i]
+        sums = lax.fori_loop(8 * k, 8 * k + 8, absorb, sums)
 
     sums = jnp.transpose(jnp.concatenate(sums, axis=0))
     for k in range(4):
@@ -263,29 +258,43 @@
     def _():
         pltpu.make_async_copy(tx_s.at[b_lo], rx_s.at[b_lo], s_recv).start()
 
+    def s_send(to):
+        pltpu.make_async_remote_copy(
+            src_ref=tx_s.at[to],
+            dst_ref=rx_s.at[b_lo],
+            send_sem=s_send_sem,
+            recv_sem=s_recv,
+            device_id=(32 * a + to, b_hi),
+            device_id_type=MESH,
+        ).start()
+
     def s_sends(to_late):
-        def step(j, carry):
-            to = (b_lo + j) & 31
-            wanted = is_late(32 * a + to) == to_late
-
-            @pl.when(jnp.logical_and(wanted, jnp.logical_not(jnp.logical_and(mine, j == 0))))
+        @pl.when(a == 2)
+        def _():
+            def step(to, carry):
+                wanted = is_late(64 + to) == to_late
+
+                @pl.when(jnp.logical_and(wanted, jnp.logical_not(jnp.logical_and(mine, to == b_lo))))
+                def _():
+                    s_send(to)
+
+                return carry
+
+            lax.fori_loop(0, 32, step, 0)
+
+        @pl.when(a == 3 if to_late else a < 2)
+        def _():
+            @pl.when(jnp.logical_not(mine))
             def _():
-                pltpu.make_async_remote_copy(
-                    src_ref=tx_s.at[to],
-                    dst_ref=rx_s.at[b_lo],
-                    send_sem=s_send,
-                    recv_sem=s_recv,
-                    device_id=(32 * a + to, b_hi),
-                    device_id_type=MESH,
-                ).start()
-
-            return carry
-
-        lax.fori_loop(0, 32, step, 0)
-
-    @pl.when(a < 3)
-    def _():
-        s_sends(False)
+                s_send(b_lo)
+
+            def step(j, carry):
+                s_send((b_lo + j) & 31)
+                return carry
+
+            lax.fori_loop(1, 32, step, 0, unroll=31)
+
+    s_sends(False)
 
     @pl.when(core == 0)
     def _():
@@ -296,19 +305,30 @@
         pl.semaphore_wait(bar, LATE + 1 - self_counted)
         pl.semaphore_signal(pair_sem, inc=1, device_id=sibling, device_id_type=MESH)
 
-    @pl.when(jnp.logical_not(jnp.logical_and(mine, late)))
-    def _():
-        c_copy(late_to(0)).start()
+    @pl.when(jnp.logical_not(jnp.logical_and(mine, b >= 96)))
+    def _():
+        c_copy(96 + b_lo).start()
 
     def late_step(j, carry):
-        c_copy(late_to(j)).start()
+        c_copy(96 + (j ^ b_lo)).start()
         return carry
 
-    lax.fori_loop(1, LATE, late_step, 0, unroll=5)
-
-    @pl.when(a >= 2)
-    def _():
-        s_sends(True)
+    lax.fori_loop(1, 32, late_step, 0, unroll=31)
+    between([j for j in range(32) if j & 15 >= 4])
+
+    s_sends(True)
+
+    weight = [prm[3, 8 * i : 8 * i + 8, :] for i in range(16)]
+
+    def radiate(k, carry):
+        k = pl.multiple_of(8 * k, 8)
+        for u in range(8):
+            q = jnp.broadcast_to(1.0 + 0.2 * t_s[pl.ds(k + u, 1), :], (8, 128))
+            for i in range(16):
+                emit[k + u, 8 * i : 8 * i + 8, :] = weight[i] * q
+        return carry
+
+    lax.fori_loop(0, 16, radiate, 0)
 
     m, n = iota((256, 512), 0), iota((256, 512), 1)
     slot = m & 127
@@ -318,8 +338,12 @@
     got = jnp.transpose(rx_c[:, 0, :])
     both = jnp.concatenate([got[0:32], got[32:64]], axis=1).astype(BF16)
     cond = dot(both, pick, ((1,), (0,)))
+    c_sums = jnp.zeros((1, 128), F32)
     for k in range(4):
-        c_s[32 * k : 32 * k + 32, :] = cond[:, 128 * k : 128 * k + 128]
+        part = cond[:, 128 * k : 128 * k + 128]
+        c_s[32 * k : 32 * k + 32, :] = part
+        c_above[k] = jnp.broadcast_to(c_sums, (8, 128))
+        c_sums = c_sums + jnp.sum(part, axis=0, keepdims=True)
     sun = got[64:72]
     first = sun[0:1] + sun[1:2] + sun[2:3]
     second = jnp.broadcast_to(sun[3:4] + sun[4:5] + sun[5:6], (8, 128))
@@ -339,9 +363,6 @@
         )
 
     def levels(first, trans):
-        rows_q = [
-            jnp.broadcast_to(1.0 + 0.2 * t_s[pl.ds(first + u, 1), :], (8, 128)) for u in range(UNROLL)
-        ]
         rows_c = [jnp.broadcast_to(c_s[pl.ds(first + u, 1), :], (8, 128)) for u in range(UNROLL)]
         totals = [None] * UNROLL
         trans = list(trans)
@@ -349,34 +370,40 @@
             for i in range(16):
                 rows = slice(8 * i, 8 * i + 8)
                 e = jnp.exp2(prm[0, rows, :] * (xs[first + u, rows, :] + rows_c[u]))
-                term = (1.0 - e) * (trans[i] - prm[3, rows, :] * rows_q[u])
+                term = (1.0 - e) * (trans[i] - emit[first + u, rows, :])
                 trans[i] = trans[i] * e
                 totals[u] = term if i == 0 else totals[u] + term
         for u in range(UNROLL):
             acc[first + u] = totals[u]
         return tuple(trans)
 
-    trans = tuple(prm[2, 8 * i : 8 * i + 8, :] * sun for i in range(16))
-    def quarter(part, trans):
+    def quarter(step, carry):
+        part = (a + jnp.where(step == 0, 2, jnp.where(step == 1, 1, jnp.where(step == 2, 3, 0)))) & 3
         first = pl.multiple_of(32 * part, 32)
-        trans = lax.fori_loop(
-            0, 32 // UNROLL, lambda k, v: levels(first + UNROLL * k, v), trans
+        c = c_above[part]
+        trans = []
+        for i in range(16):
+            rows = slice(8 * i, 8 * i + 8)
+            depth = prm[0, rows, :] * (above[part, rows, :] + c)
+            trans.append(prm[2, rows, :] * sun * jnp.exp2(depth))
+        lax.fori_loop(
+            0, 32 // UNROLL, lambda k, v: levels(pl.multiple_of(first + UNROLL * k, UNROLL), v), tuple(trans)
         )
         heat = 0.0625 * jnp.sum(acc[pl.ds(first, 32)], axis=1)
         heat = heat + pltpu.roll(heat, 64, 1)
 
-        @pl.when(a == part)
+        @pl.when(step == 3)
         def _():
             rx_h[part] = heat
 
-        @pl.when(a != part)
+        @pl.when(step < 3)
         def _():
             tx_h[part] = heat
             h_copy(part).start()
 
-        return trans
-
-    lax.fori_loop(0, 4, quarter, trans)
+        return carry
+
+    lax.fori_loop(0, 4, quarter, 0)
 
     await_bytes(rx_s, s_recv)
     lane, row = iota((32, 128), 1), iota((32, 128), 0)
@@ -416,12 +443,12 @@
     @pl.when(mine)
     def _():
         await_bytes(tx_c.at[pl.ds(0, 127)], c_send)
-        await_bytes(tx_s.at[pl.ds(0, 31)], s_send)
+        await_bytes(tx_s.at[pl.ds(0, 31)], s_send_sem)
 
     @pl.when(jnp.logical_not(mine))
     def _():
         await_bytes(tx_c, c_send)
-        await_bytes(tx_s, s_send)
+        await_bytes(tx_s, s_send_sem)
 
 
 def place(heat_in, surf_in, heat_out, surf_out, sem):
@@ -470,9 +497,12 @@
             pltpu.VMEM((128, 128), F32),
             pltpu.VMEM((128, 128), F32),
             pltpu.VMEM((128, 128), F32),
+            pltpu.VMEM((4, 8, 128), F32),
             pltpu.VMEM((4, 128, 128), F32),
             pltpu.VMEM((128, 8, 128), F32),
             pltpu.VMEM((128, 128, 128), F32),
+            pltpu.VMEM((128, 128, 128), F32),
+            pltpu.VMEM((4, 128, 128), F32),
             pltpu.SemaphoreType.DMA((9,)),
         ]
         + [pltpu.SemaphoreType.DMA] * 8

time: 30.4 us -> 29.6 us (0.974)
  the two profiles are of different devices: /device:TPU:398 before, /device:TPU:3 now
where the time goes in v5:
time: 29.6 us; the launch traced here: 29.4 us
  Pallas kernels  28.8 us (97%)
  between operations  0.64 us (2%)
    pallas_call x1, Pallas kernels, shards(): pl.pallas_call(kernel, out_shape=(jax.ShapeDtypeStruct((32, 256), F32), j...  28.2 us
    pallas_call x1, Pallas kernels, shards(): pl.pallas_call(place, out_shape=(jax.ShapeDtypeStruct((32, 256), F32), ja...  0.64 us

profile of v5, /device:TPU:3, one launch (start us, length us, event | category | flops | bytes accessed | tf_op | source)
XLA Modules:
  0.0 29.4 jit_solution(10290551293629763501)
XLA Ops:
  0.6 28.2 %shard_map.104 = (f32[32,256]{1,0:T(8,128)S(1)}, f32[1,64]{1,0:T(1,128)S(1)}) custom-call(bf16[32,256]{1,0:T(8,128)(2,1)} %bitcast.11, bf16[32,256]{1,0:T(8,128)(2,1)} %bitcast.12, bf16[32,256]{1,0:T(8,128)(2,1)} %bitcast.13, f32[1,256]{1,0:T(1,128)} %bitcast.14, s32[1,256]{1,0:T(1,128)} %bitcast.15, f32[1,64]{1,0:T(1,128)} %bitcast.16, f32[1,64]{1,0:T(1,128)} %bitcast.17, ...), custom_call_target="tpu_custom_call" | custom-call | tf_op jit(solution)/shard_map/pallas_call | solution.py:470
  28.8 0.6 %shard_map.105 = (f32[32,256]{1,0:T(8,128)}, f32[1,64]{1,0:T(1,128)}) custom-call(f32[32,256]{1,0:T(8,128)S(1)} %get-tuple-element.6.heat_in, f32[1,64]{1,0:T(1,128)S(1)} %get-tuple-element.7.surf_in), custom_call_target="tpu_custom_call" | custom-call | tf_op jit(solution)/shard_map/pallas_call | solution.py:529

commit v6 on v5

--- a/solution.py
+++ b/solution.py
@@ -45,7 +45,7 @@
     t_in, w_in, c_in, mu_in, g_in, op_in, tp_in, sw_in, tw_in,
     tx_c, rx_c, tx_g, rx_g, tx_h, rx_h, tx_s, rx_s,
     onehot, t_s, w_s, c_s, c_above, prm, acc, xs, emit, above,
-    in_sem, c_send, c_recv, g_send, g_recv, h_send, h_recv, s_send_sem, s_recv, pair_sem,
+    in_sem, c_send, c_recv, g_send, g_recv, h_send, h_recv, s_send_sem, s_recv, line_sem, early_sem, late_sem,
 ):
     b = lax.axis_index("blk")
     a = lax.axis_index("ga")
@@ -54,6 +54,10 @@
     core = b & 1
     late = is_late(b)
     sibling = (b ^ 1, a)
+    line = [(b, a ^ k) for k in range(1, 4)] + [(b ^ 1, a ^ k) for k in range(4)]
+    counts_early = jnp.logical_and(core == 0, mine)
+    counts_late = jnp.logical_and(core == 1, (a ^ 1) == b_hi)
+    counts = jnp.logical_or(counts_early, counts_late)
 
     loads = [
         pltpu.make_async_copy(src, dst, in_sem.at[i])
@@ -72,24 +76,20 @@
     def greet(dev):
         pl.semaphore_signal(bar, inc=1, device_id=dev, device_id_type=MESH)
 
-    greet(sibling)
-    for k in range(1, 4):
-        greet((b & 126, (a + k) & 3))
-    told = jnp.where(late, 1, 0)
-    told_self = jnp.logical_and(mine, core == told)
-
-    def announce(j):
-        greet((32 * a + told + ((2 * (j >> 2)) ^ (b_lo & 30)), (a ^ j) & 3))
-
-    @pl.when(jnp.logical_not(told_self))
+    for dev in line:
+        greet(dev)
+    self_counted = jnp.logical_and(counts_early, jnp.logical_not(late))
+    told = jnp.where(late, a ^ 1, a)
+
+    def announce(m):
+        greet((32 * a + ((2 * m) ^ (b_lo & 30)) + jnp.where(late, 1, 0), told))
+
+    for m in (4, 12, 5, 13, 3, 11, 6, 14, 2, 10, 7, 15, 1, 9, 8):
+        announce(m)
+
+    @pl.when(jnp.logical_not(self_counted))
     def _():
         announce(0)
-
-    def announce_step(j, carry):
-        announce(j)
-        return carry
-
-    lax.fori_loop(1, 64, announce_step, 0, unroll=9)
 
     loads[0].wait()
     loads[1].wait()
@@ -149,16 +149,21 @@
         for half in range(2):
             tx_g[2 * k + half, 64:80, :] = full.astype(BF16)
 
-    self_counted = jnp.where(told_self, 1, 0)
-
-    @pl.when(core == 0)
-    def _():
-        pl.semaphore_wait(bar, EARLY + 7 - self_counted)
-        pl.semaphore_signal(pair_sem, inc=1, device_id=sibling, device_id_type=MESH)
-
-    @pl.when(core == 1)
-    def _():
-        pl.semaphore_wait(pair_sem, 1)
+    def tell(sem, devices):
+        for dev in devices:
+            pl.semaphore_signal(sem, inc=1, device_id=dev, device_id_type=MESH)
+
+    @pl.when(counts)
+    def _():
+        pl.semaphore_wait(line_sem, 1)
+
+    @pl.when(jnp.logical_not(counts))
+    def _():
+        pl.semaphore_wait(bar, 7)
+
+    @pl.when(jnp.logical_or(jnp.logical_and(core == 1, mine), jnp.logical_and(core == 0, (a ^ 1) == b_hi)))
+    def _():
+        tell(line_sem, [sibling])
 
     def c_copy(to):
         return pltpu.make_async_remote_copy(
@@ -184,19 +189,30 @@
     for k in range(1, 4):
         g_copy(k).start()
 
+    @pl.when(counts_early)
+    def _():
+        pl.semaphore_wait(bar, EARLY + 7 - jnp.where(self_counted, 1, 0))
+        tell(early_sem, line)
+
+    @pl.when(jnp.logical_not(counts_early))
+    def _():
+        pl.semaphore_wait(early_sem, 1)
+
     @pl.when(mine)
     def _():
         pltpu.make_async_copy(tx_c.at[b], rx_c.at[a * 32 + b_lo], c_recv).start()
 
+    def early_step(j, carry):
+        c_copy(j ^ 40 ^ (b & 63)).start()
+        return carry
+
+    lax.fori_loop(0, 40, early_step, 0, unroll=8)
+
     @pl.when(jnp.logical_not(jnp.logical_and(mine, b < 64)))
     def _():
         c_copy(b & 63).start()
 
-    def early_step(j, carry):
-        c_copy(j ^ (b & 63)).start()
-        return carry
-
-    lax.fori_loop(1, 64, early_step, 0, unroll=9)
+    lax.fori_loop(41, 64, early_step, 0, unroll=23)
 
     def between(members):
         for j in members:
@@ -296,24 +312,26 @@
 
     s_sends(False)
 
-    @pl.when(core == 0)
-    def _():
-        pl.semaphore_wait(pair_sem, 1)
-
-    @pl.when(core == 1)
-    def _():
-        pl.semaphore_wait(bar, LATE + 1 - self_counted)
-        pl.semaphore_signal(pair_sem, inc=1, device_id=sibling, device_id_type=MESH)
+    @pl.when(counts_late)
+    def _():
+        pl.semaphore_wait(bar, LATE + 7)
+        tell(late_sem, line)
+
+    @pl.when(jnp.logical_not(counts_late))
+    def _():
+        pl.semaphore_wait(late_sem, 1)
+
+    def late_step(j, carry):
+        c_copy(96 + (j ^ 8 ^ b_lo)).start()
+        return carry
+
+    lax.fori_loop(0, 8, late_step, 0, unroll=8)
 
     @pl.when(jnp.logical_not(jnp.logical_and(mine, b >= 96)))
     def _():
         c_copy(96 + b_lo).start()
 
-    def late_step(j, carry):
-        c_copy(96 + (j ^ b_lo)).start()
-        return carry
-
-    lax.fori_loop(1, 32, late_step, 0, unroll=31)
+    lax.fori_loop(9, 32, late_step, 0, unroll=23)
     between([j for j in range(32) if j & 15 >= 4])
 
     s_sends(True)
@@ -506,7 +524,7 @@
             pltpu.SemaphoreType.DMA((9,)),
         ]
         + [pltpu.SemaphoreType.DMA] * 8
-        + [pltpu.SemaphoreType.REGULAR],
+        + [pltpu.SemaphoreType.REGULAR] * 3,
         compiler_params=pltpu.CompilerParams(
             collective_id=0, has_side_effects=True, vmem_limit_bytes=32 * 1024 * 1024
         ),

time: 29.6 us -> 29.1 us (0.983)
  the two profiles are of different devices: /device:TPU:3 before, /device:TPU:1 now
where the time goes in v6:
time: 29.1 us; the launch traced here: 29 us
  Pallas kernels  28.3 us (97%)
  between operations  0.64 us (2%)
    pallas_call x1, Pallas kernels, shards(): pl.pallas_call(kernel, out_shape=(jax.ShapeDtypeStruct((32, 256), F32), j...  27.7 us
    pallas_call x1, Pallas kernels, shards(): pl.pallas_call(place, out_shape=(jax.ShapeDtypeStruct((32, 256), F32), ja...  0.64 us

profile of v6, /device:TPU:1, one launch (start us, length us, event | category | flops | bytes accessed | tf_op | source)
XLA Modules:
  0.0 29.0 jit_solution(16814349112142687645)
XLA Ops:
  0.6 27.7 %shard_map.104 = (f32[32,256]{1,0:T(8,128)S(1)}, f32[1,64]{1,0:T(1,128)S(1)}) custom-call(bf16[32,256]{1,0:T(8,128)(2,1)} %bitcast.11, bf16[32,256]{1,0:T(8,128)(2,1)} %bitcast.12, bf16[32,256]{1,0:T(8,128)(2,1)} %bitcast.13, f32[1,256]{1,0:T(1,128)} %bitcast.14, s32[1,256]{1,0:T(1,128)} %bitcast.15, f32[1,64]{1,0:T(1,128)} %bitcast.16, f32[1,64]{1,0:T(1,128)} %bitcast.17, ...), custom_call_target="tpu_custom_call" | custom-call | tf_op jit(solution)/shard_map/pallas_call | solution.py:488
  28.3 0.6 %shard_map.105 = (f32[32,256]{1,0:T(8,128)}, f32[1,64]{1,0:T(1,128)}) custom-call(f32[32,256]{1,0:T(8,128)S(1)} %get-tuple-element.6.heat_in, f32[1,64]{1,0:T(1,128)S(1)} %get-tuple-element.7.surf_in), custom_call_target="tpu_custom_call" | custom-call | tf_op jit(solution)/shard_map/pallas_call | solution.py:547

commit v7 on v6

--- a/solution.py
+++ b/solution.py
@@ -114,6 +114,18 @@
     pick = ones_where((col & 255) == 2 * row + (col >> 8))
     tx_c[:, 0, :] = dot(pick, laid, ((1,), (1,)))
 
+    def tell(sem, devices):
+        for dev in devices:
+            pl.semaphore_signal(sem, inc=1, device_id=dev, device_id_type=MESH)
+
+    def count_early():
+        pl.semaphore_wait(bar, EARLY + 7 - jnp.where(self_counted, 1, 0))
+        tell(early_sem, line)
+
+    @pl.when(jnp.logical_and(counts_early, b_hi >= 2))
+    def _():
+        count_early()
+
     loads[2].wait()
     groups = g_in[...]
     member = groups == iota((128, 256), 0)
@@ -126,9 +138,10 @@
     onehot[...] = hot
     loads[3].wait()
     loads[4].wait()
-    moved = dot(jnp.concatenate([t_in[...], w_in[...]], axis=0), hot, ((1,), (1,))).astype(BF16)
+    moved = dot(jnp.concatenate([t_in[...], w_in[...]], axis=0), hot, ((1,), (1,)))
+    moved = jnp.where((iota((32, 512), 1) & 64) == 0, moved[0:32], moved[32:64]).astype(BF16)
     for k in range(4):
-        tx_g[k, 0:64, :] = moved[:, 128 * k : 128 * k + 128]
+        tx_g[k, 0:32, :] = moved[:, 128 * k : 128 * k + 128]
 
     for load in loads[5:]:
         load.wait()
@@ -147,11 +160,7 @@
         for s, part in enumerate(split3(v)):
             full = jnp.where(row == 12 + s, part.astype(F32), full)
         for half in range(2):
-            tx_g[2 * k + half, 64:80, :] = full.astype(BF16)
-
-    def tell(sem, devices):
-        for dev in devices:
-            pl.semaphore_signal(sem, inc=1, device_id=dev, device_id_type=MESH)
+            tx_g[2 * k + half, 32:48, :] = full.astype(BF16)
 
     @pl.when(counts)
     def _():
@@ -189,10 +198,9 @@
     for k in range(1, 4):
         g_copy(k).start()
 
-    @pl.when(counts_early)
-    def _():
-        pl.semaphore_wait(bar, EARLY + 7 - jnp.where(self_counted, 1, 0))
-        tell(early_sem, line)
+    @pl.when(jnp.logical_and(counts_early, b_hi < 2))
+    def _():
+        count_early()
 
     @pl.when(jnp.logical_not(counts_early))
     def _():
@@ -230,9 +238,12 @@
 
     await_bytes(rx_g.at[pl.ds(0, 3)], g_recv)
     for k in range(4):
-        t_s[32 * k : 32 * k + 32, :] = rx_g[k, 0:32, :].astype(F32)
-        w_s[32 * k : 32 * k + 32, :] = rx_g[k, 32:64, :].astype(F32)
-    parts = [rx_g[k, 64:80, :].astype(F32) for k in range(4)]
+        both = rx_g[k, 0:32, :].astype(F32)
+        other = pltpu.roll(both, 64, 1)
+        in_first = iota((32, 128), 1) < 64
+        t_s[32 * k : 32 * k + 32, :] = jnp.where(in_first, both, other)
+        w_s[32 * k : 32 * k + 32, :] = jnp.where(in_first, other, both)
+    parts = [rx_g[k, 32:48, :].astype(F32) for k in range(4)]
     parts = [parts[0] + parts[1], parts[2] + parts[3]]
     m, n = iota((32, 512), 0), iota((32, 512), 1)
     pick = jnp.logical_and(
@@ -396,7 +407,13 @@
         return tuple(trans)
 
     def quarter(step, carry):
-        part = (a + jnp.where(step == 0, 2, jnp.where(step == 1, 1, jnp.where(step == 2, 3, 0)))) & 3
+        def turn(*parts):
+            part = parts[3]
+            for k in range(3):
+                part = jnp.where(step == k, parts[k], part)
+            return part
+
+        part = jnp.where(a == 0, turn(2, 1, 3, 0), jnp.where(a == 1, turn(0, 3, 2, 1), jnp.where(a == 2, turn(0, 1, 3, 2), step)))
         first = pl.multiple_of(32 * part, 32)
         c = c_above[part]
         trans = []
@@ -505,8 +522,8 @@
             pltpu.VMEM((1, 64), F32),
             pltpu.VMEM((128, 1, 128), F32),
             pltpu.VMEM((128, 1, 128), F32),
-            pltpu.VMEM((4, 80, 128), BF16),
-            pltpu.VMEM((4, 80, 128), BF16),
+            pltpu.VMEM((4, 48, 128), BF16),
+            pltpu.VMEM((4, 48, 128), BF16),
             pltpu.VMEM((4, 32, 128), F32),
             pltpu.VMEM((4, 32, 128), F32),
             pltpu.VMEM((32, 4, 128), F32),

time: 29.1 us -> 28.5 us (0.979)
  Pallas kernels: 28.3 us -> 27.6 us
    pallas_call x1, Pallas kernels: 27.7 us -> 27 us  [shards(): pl.pallas_call(kernel, out_shape=(jax.ShapeDtypeStruct((32, 256), F32), j...]
where the time goes in v7:
time: 28.5 us; the launch traced here: 28.3 us
  Pallas kernels  27.6 us (97%)
  between operations  0.64 us (2%)
    pallas_call x1, Pallas kernels, shards(): pl.pallas_call(kernel, out_shape=(jax.ShapeDtypeStruct((32, 256), F32), j...  27 us
    pallas_call x1, Pallas kernels, shards(): pl.pallas_call(place, out_shape=(jax.ShapeDtypeStruct((32, 256), F32), ja...  0.64 us

profile of v7, /device:TPU:1, one launch (start us, length us, event | category | flops | bytes accessed | tf_op | source)
XLA Modules:
  0.0 28.3 jit_solution(18065393808116953039)
XLA Ops:
  0.6 27.0 %shard_map.104 = (f32[32,256]{1,0:T(8,128)S(1)}, f32[1,64]{1,0:T(1,128)S(1)}) custom-call(bf16[32,256]{1,0:T(8,128)(2,1)} %bitcast.11, bf16[32,256]{1,0:T(8,128)(2,1)} %bitcast.12, bf16[32,256]{1,0:T(8,128)(2,1)} %bitcast.13, f32[1,256]{1,0:T(1,128)} %bitcast.14, s32[1,256]{1,0:T(1,128)} %bitcast.15, f32[1,64]{1,0:T(1,128)} %bitcast.16, f32[1,64]{1,0:T(1,128)} %bitcast.17, ...), custom_call_target="tpu_custom_call" | custom-call | tf_op jit(solution)/shard_map/pallas_call | solution.py:505
  27.6 0.6 %shard_map.105 = (f32[32,256]{1,0:T(8,128)}, f32[1,64]{1,0:T(1,128)}) custom-call(f32[32,256]{1,0:T(8,128)S(1)} %get-tuple-element.6.heat_in, f32[1,64]{1,0:T(1,128)S(1)} %get-tuple-element.7.surf_in), custom_call_target="tpu_custom_call" | custom-call | tf_op jit(solution)/shard_map/pallas_call | solution.py:564

commit v8 on v7

--- a/solution.py
+++ b/solution.py
@@ -426,6 +426,7 @@
         )
         heat = 0.0625 * jnp.sum(acc[pl.ds(first, 32)], axis=1)
         heat = heat + pltpu.roll(heat, 64, 1)
+        heat = jnp.where(iota((16, 128), 1) < 64, heat[0:16], heat[16:32])
 
         @pl.when(step == 3)
         def _():
@@ -468,7 +469,8 @@
 
     await_bytes(rx_h.at[pl.ds(0, 3)], h_recv)
     heat = jnp.concatenate([rx_h[k] for k in range(4)], axis=1)
-    heat = jnp.where((iota((32, 512), 1) & 127) < 64, heat, 0.0)
+    in_first = (iota((16, 512), 1) & 64) == 0
+    heat = jnp.concatenate([jnp.where(in_first, heat, 0.0), jnp.where(in_first, 0.0, heat)], axis=0)
     heat = dot(jnp.concatenate(split3(heat), axis=0), onehot[...], ((1,), (0,)))
     heat_ref[...] = heat[0:32] + heat[32:64] + heat[64:96]
 
@@ -524,8 +526,8 @@
             pltpu.VMEM((128, 1, 128), F32),
             pltpu.VMEM((4, 48, 128), BF16),
             pltpu.VMEM((4, 48, 128), BF16),
-            pltpu.VMEM((4, 32, 128), F32),
-            pltpu.VMEM((4, 32, 128), F32),
+            pltpu.VMEM((4, 16, 128), F32),
+            pltpu.VMEM((4, 16, 128), F32),
             pltpu.VMEM((32, 4, 128), F32),
             pltpu.VMEM((32, 4, 128), F32),
             pltpu.VMEM((512, 256), BF16),

time: 28.5 us -> 28.4 us (level)
  no operation moved by 1% of the time
where the time goes in v8:
time: 28.4 us; the launch traced here: 28.2 us
  Pallas kernels  27.5 us (97%)
  between operations  0.64 us (2%)
    pallas_call x1, Pallas kernels, shards(): pl.pallas_call(kernel, out_shape=(jax.ShapeDtypeStruct((32, 256), F32), j...  26.9 us
    pallas_call x1, Pallas kernels, shards(): pl.pallas_call(place, out_shape=(jax.ShapeDtypeStruct((32, 256), F32), ja...  0.64 us

profile of v8, /device:TPU:1, one launch (start us, length us, event | category | flops | bytes accessed | tf_op | source)
XLA Modules:
  0.0 28.2 jit_solution(5780210929659148958)
XLA Ops:
  0.6 26.9 %shard_map.104 = (f32[32,256]{1,0:T(8,128)S(1)}, f32[1,64]{1,0:T(1,128)S(1)}) custom-call(bf16[32,256]{1,0:T(8,128)(2,1)} %bitcast.11, bf16[32,256]{1,0:T(8,128)(2,1)} %bitcast.12, bf16[32,256]{1,0:T(8,128)(2,1)} %bitcast.13, f32[1,256]{1,0:T(1,128)} %bitcast.14, s32[1,256]{1,0:T(1,128)} %bitcast.15, f32[1,64]{1,0:T(1,128)} %bitcast.16, f32[1,64]{1,0:T(1,128)} %bitcast.17, ...), custom_call_target="tpu_custom_call" | custom-call | tf_op jit(solution)/shard_map/pallas_call | solution.py:507
  27.5 0.6 %shard_map.105 = (f32[32,256]{1,0:T(8,128)}, f32[1,64]{1,0:T(1,128)}) custom-call(f32[32,256]{1,0:T(8,128)S(1)} %get-tuple-element.6.heat_in, f32[1,64]{1,0:T(1,128)S(1)} %get-tuple-element.7.surf_in), custom_call_target="tpu_custom_call" | custom-call | tf_op jit(solution)/shard_map/pallas_call | solution.py:566
